TPU v7x, 32 devices: a whole 2x2x4 slice. The times are simulated.
32 devices in a mesh: dp: 8 (over y, x, core), tensor: 4 (over z).
Axes of the slice: x: 2, y: 2, z: 4, core: 2. Of those that a mesh axis runs over, the one named last changes fastest.
Arguments:
- hidden_in: bfloat16 [8192, 2560], P(('dp', 'tensor')), may hold values from -6 to 6
- attention_gain: bfloat16 [2560], P(('dp', 'tensor')), may hold values from 0.25 to 1.75
- query_down: bfloat16 [2560, 768], P(('dp', 'tensor')), may hold values from -0.125 to 0.125
- query_norm: bfloat16 [768], P(('dp', 'tensor')), may hold values from 0.25 to 1.75
- latent_down: bfloat16 [2560, 288], P(('dp', 'tensor')), may hold values from -0.125 to 0.125
- latent_norm: bfloat16 [256], P(('dp', 'tensor')), may hold values from 0.25 to 1.75
- query_up: bfloat16 [768, 3840], P('dp', 'tensor'), may hold values from -0.21875 to 0.21875
- latent_up: bfloat16 [256, 5120], P('dp', 'tensor'), may hold values from -0.375 to 0.375
- output_weight: bfloat16 [2560, 2560], P('tensor', 'dp'), may hold values from -2 to 2
- feed_gain: bfloat16 [2560], P(('dp', 'tensor')), may hold values from 0.25 to 1.75
- gate_weight: bfloat16 [2560, 6400], P('dp', 'tensor'), may hold values from -0.125 to 0.125
- up_weight: bfloat16 [2560, 6400], P('dp', 'tensor'), may hold values from -0.125 to 0.125
- down_weight: bfloat16 [6400, 2560], P('tensor', 'dp'), may hold values from -0.875 to 0.875
- cotangent: bfloat16 [8192, 2560], P(('dp', 'tensor')), may hold values from -6 to 6
- document_lengths: int32 [8, 4], P('dp'), may hold values from 0 to 1024, as said below
Outputs:
- layer_output: bfloat16 [8192, 2560], P(('dp', 'tensor'))
- input_gradient: bfloat16 [8192, 2560], P(('dp', 'tensor'))
- attention_gain_gradient: float32 [2560], P(('dp', 'tensor'))
- query_down_gradient: float32 [2560, 768], P(('dp', 'tensor'))
- query_norm_gradient: float32 [768], P(('dp', 'tensor'))
- latent_down_gradient: float32 [2560, 288], P(('dp', 'tensor'))
- latent_norm_gradient: float32 [256], P(('dp', 'tensor'))
- query_up_gradient: float32 [768, 3840], P('dp', 'tensor')
- latent_up_gradient: float32 [256, 5120], P('dp', 'tensor')
- output_weight_gradient: float32 [2560, 2560], P('tensor', 'dp')
- feed_gain_gradient: float32 [2560], P(('dp', 'tensor'))
- gate_gradient: float32 [2560, 6400], P('dp', 'tensor')
- up_gradient: float32 [2560, 6400], P('dp', 'tensor')
- down_gradient: float32 [6400, 2560], P('tensor', 'dp')
Inputs may be any that keep to these rules, and one draw needn't show every extreme that they name: `document_lengths`: each row holds the lengths of the 4 documents of one data group in order; their sum is at most 1024 and the slots after it are padding, a segment of its own. Documents may be empty. In every group one document is longer than 768, and some group holds a single document of 1024 tokens.
All inputs are finite; a program needn't handle non-finite values.
Results may differ from a plain program's by a relative error of at most 0.02.
Values may be sent and summed in bfloat16 or wider, within the bound.
No kernel may reach another device: no remote copies, remote signals or barrier semaphores. Data moves between devices by JAX's collectives and lax.ppermute only.
A program may use at most 256 MiB of HBM per device.

v0:
```python
import math, functools
import jax, jax.numpy as jnp
from jax import lax
from jax.experimental import pallas as pl
from jax.experimental.pallas import tpu as pltpu
from jax.sharding import PartitionSpec as P

KVR, ROPE, NOPE, VD = 256, 32, 64, 64
LANES = 128
softmax_scale = 1.0 / math.sqrt(NOPE + ROPE)
log2_scale = softmax_scale / math.log(2.0)


def nt(left, right):
    return lax.dot_general(left, right, (((1,), (1,)), ((), ())), preferred_element_type=jnp.float32)


def nn(left, right):
    return lax.dot_general(left, right, (((1,), (0,)), ((), ())), preferred_element_type=jnp.float32)


def tn(left, right):
    return lax.dot_general(left, right, (((0,), (0,)), ((), ())), preferred_element_type=jnp.float32)


def attention_forward_kernel(rank, block, latents, up_q, up_kv, cosine, sine_left, sine_right, segment_col, segment_row, attended, queries, expanded, log_total):
    pair = pl.program_id(0)
    group = latents.shape[0]
    lane = lax.broadcasted_iota(jnp.int32, (1, LANES), 1)
    rotary = latents[:, rank + KVR :].astype(jnp.float32)

    @pl.when(pair == 0)
    def _():
        log_total[...] = jnp.zeros_like(log_total)

    found = []
    for half in range(2):
        columns = slice(half * LANES, (half + 1) * LANES)
        raw = nn(latents[:, :rank], up_q[:, columns])
        turned = raw * cosine[...] + pltpu.roll(raw, LANES - ROPE // 2, 1) * sine_left[...] + pltpu.roll(raw, ROPE // 2, 1) * sine_right[...]
        query = turned.astype(jnp.bfloat16)
        queries[:, columns] = query
        both = nn(latents[:, rank : rank + KVR], up_kv[:, columns])
        key = jnp.where(lane < NOPE, both, rotary).astype(jnp.bfloat16)
        both = both.astype(jnp.bfloat16)
        expanded[:, columns] = both
        outs, sums = [], []
        for begin in range(0, group, block):
            end = begin + block
            scores = nt(query[begin:end], key[:end]) * log2_scale
            allowed = segment_col[begin:end, :] == segment_row[:, :end]
            row = lax.broadcasted_iota(jnp.int32, (block, end), 0) + begin
            column = lax.broadcasted_iota(jnp.int32, (block, end), 1)
            scores = jnp.where(allowed & (column <= row), scores, -1e30)
            peak = jnp.max(scores, axis=-1, keepdims=True)
            weights = jnp.exp2(scores - peak)
            total = jnp.sum(weights, axis=-1, keepdims=True)
            outs.append(nn(weights.astype(jnp.bfloat16), both[:end]) / total)
            sums.append(peak + jnp.log2(total))
        found.append(jnp.concatenate(outs, axis=0))
        log_total[...] = jnp.where(lane == 2 * pair + half, jnp.concatenate(sums, axis=0), log_total[...])
    attended[...] = jnp.where(lane < VD, pltpu.roll(found[0], VD, 1), found[1]).astype(jnp.bfloat16)


def attention_backward_kernel(block, queries, expanded, rotary_in, cosine, sine_left, sine_right, segment_col, segment_row, log_total, grad, query_grad, expanded_grad, rotary_grad, key_sum, value_sum):
    pair = pl.program_id(0)
    group = queries.shape[0]
    lane = lax.broadcasted_iota(jnp.int32, (1, LANES), 1)
    rotary = rotary_in[...].astype(jnp.float32)

    @pl.when(pair == 0)
    def _():
        rotary_grad[...] = jnp.zeros_like(rotary_grad)

    grads = grad[...].astype(jnp.float32)
    for half in range(2):
        columns = slice(half * LANES, (half + 1) * LANES)
        query = queries[:, columns]
        both = expanded[:, columns]
        key = jnp.where(lane < NOPE, both.astype(jnp.float32), rotary).astype(jnp.bfloat16)
        out_grad = pltpu.roll(grads, VD, 1) if half == 0 else grads
        out_grad = jnp.where(lane < NOPE, 0.0, out_grad).astype(jnp.bfloat16)
        log_row = log_total[pl.ds(2 * pair + half, 1), :]
        parts = []
        for begin in reversed(range(0, group, block)):
            end = begin + block
            scores = nt(key[:end], query[begin:end]) * log2_scale
            allowed = segment_col[:end, :] == segment_row[:, begin:end]
            row = lax.broadcasted_iota(jnp.int32, (end, block), 0)
            column = lax.broadcasted_iota(jnp.int32, (end, block), 1) + begin
            probs = jnp.where(allowed & (row <= column), jnp.exp2(scores - log_row[:, begin:end]), 0.0)
            prob_grad = nt(both[:end], out_grad[begin:end])
            center = jnp.sum(probs * prob_grad, axis=0, keepdims=True)
            score_grad = (probs * (prob_grad - center)).astype(jnp.bfloat16)
            key_part = nn(score_grad, query[begin:end])
            value_part = nn(probs.astype(jnp.bfloat16), out_grad[begin:end])
            if end == group:
                key_sum[...] = key_part
                value_sum[...] = value_part
            else:
                key_sum[:end] += key_part
                value_sum[:end] += value_part
            parts.append(tn(score_grad, key[:end]))
        found = jnp.concatenate(parts[::-1], axis=0) * softmax_scale
        back = found * cosine[...] - pltpu.roll(found, LANES - ROPE // 2, 1) * sine_left[...] - pltpu.roll(found, ROPE // 2, 1) * sine_right[...]
        query_grad[:, columns] = back.astype(jnp.bfloat16)
        keys = key_sum[...] * softmax_scale
        expanded_grad[:, columns] = jnp.where(lane < NOPE, keys, value_sum[...]).astype(jnp.bfloat16)
        rotary_grad[...] += jnp.where((lane >= NOPE) & (lane < NOPE + ROPE), keys, 0.0)


epsilon = 1e-05
residual_scale = 1.4 / math.sqrt(62.0)
rotary_base = 10000.0

RIGHT = [(i, (i + 1) % 4) for i in range(4)]
LEFT = [(i, (i - 1) % 4) for i in range(4)]
OPPOSITE = [(i, (i + 2) % 4) for i in range(4)]


def inverse_rms(values):
    return lax.rsqrt(jnp.mean(values * values, axis=-1, keepdims=True) + epsilon)


def norm_back(grad, unit, inverse, gain):
    scaled = grad * gain
    return inverse * (scaled - unit * jnp.mean(scaled * unit, axis=-1, keepdims=True))


def rotary_tables(positions, width):
    steps = jnp.arange(width // 2, dtype=jnp.float32) * (2.0 / width)
    freqs = jnp.exp(steps * -math.log(rotary_base))
    angles = positions.astype(jnp.float32)[:, None] * freqs[None, :]
    return jnp.cos(angles), jnp.sin(angles)


def layout(lengths_row, group_tokens):
    slots = jnp.arange(group_tokens, dtype=jnp.int32)
    ends = jnp.cumsum(lengths_row)
    segment = jnp.sum((slots[:, None] >= ends[None, :]).astype(jnp.int32), axis=1)
    starts = jnp.concatenate([jnp.zeros((1,), jnp.int32), ends])
    choose = segment[:, None] == jnp.arange(starts.shape[0], dtype=jnp.int32)[None, :]
    start_of = jnp.sum(jnp.where(choose, starts[None, :], 0), axis=1)
    return (segment, slots - start_of)


low, wide = jnp.bfloat16, jnp.float32
VMEM_LIMIT = 56 * 2**20


def call(kernel, name, flops, moved, **how):
    return pl.pallas_call(
        kernel,
        name=name,
        compiler_params=pltpu.CompilerParams(vmem_limit_bytes=VMEM_LIMIT),
        cost_estimate=pl.CostEstimate(flops=0, bytes_accessed=0, transcendentals=0),
        **how,
    )


def whole(*shape):
    return pl.BlockSpec(shape, lambda *i: (0,) * len(shape))


def shaped(shape, dtype):
    return jax.ShapeDtypeStruct(shape, dtype)


def place(blocks, rows_of, total):
    count, width = len(blocks), blocks[0].shape[1]

    def kernel(*refs):
        ins, out, held, done = refs[:count], refs[count], refs[count + 1 : 2 * count + 1], refs[-1]
        arrive = [pltpu.make_async_copy(ref, slot, done.at[0, k]) for k, (ref, slot) in enumerate(zip(ins, held, strict=True))]
        leave = [
            pltpu.make_async_copy(slot, out.at[pl.ds(pl.multiple_of(row, 16), slot.shape[0])], done.at[1, k])
            for k, (slot, row) in enumerate(zip(held, rows_of(), strict=True))
        ]
        for copy in arrive:
            copy.start()
        for first, second in zip(arrive, leave, strict=True):
            first.wait()
            second.start()
        for copy in leave:
            copy.wait()

    return call(
        kernel,
        "place",
        0,
        4 * total * width,
        in_specs=[pl.BlockSpec(memory_space=pl.ANY)] * count,
        out_specs=pl.BlockSpec(memory_space=pl.ANY),
        out_shape=shaped((total, width), blocks[0].dtype),
        scratch_shapes=[*[pltpu.VMEM(b.shape, b.dtype) for b in blocks], pltpu.SemaphoreType.DMA((2, count))],
    )(*blocks)


def join(target, pieces):
    row = 0
    for piece in pieces:
        target[row : row + piece.shape[0]] = piece[...]
        row += piece.shape[0]


def down_kernel(rank, places, hidden, *refs):
    pieces, (chooser, cosine, sine_left, sine_right, weights, joint, latents, gains) = refs[:-8], refs[-8:]
    for k, piece in enumerate(pieces):
        weights[pl.ds(pl.multiple_of(places[k], 16), piece.shape[0])] = piece[...]
    lane = lax.broadcasted_iota(jnp.int32, (1, LANES), 1)
    rows = weights[:, weights.shape[1] - LANES :].astype(wide).T[ROPE : ROPE + 8]
    gains[...] = rows
    chosen = nn(rows.astype(low), chooser[...])
    gains[2:3, : rank + KVR] = chosen[2:3]
    values = hidden[...].astype(wide)
    unit = values * lax.rsqrt(jnp.mean(values * values, axis=-1, keepdims=True) + epsilon)
    normed = (unit * rows[0:1]).astype(low)
    for begin in range(0, weights.shape[1], 384):
        joint[:, begin : begin + 384] = nn(normed, weights[:, begin : begin + 384])
    for begin, end in ((0, rank), (rank, rank + KVR)):
        part = joint[:, begin:end]
        latents[:, begin:end] = (part * lax.rsqrt(jnp.mean(part * part, axis=-1, keepdims=True) + epsilon) * chosen[2:3, begin:end]).astype(low)
    raw = pltpu.roll(joint[:, rank + KVR :], NOPE, 1)
    turned = raw * cosine[...] + pltpu.roll(raw, LANES - ROPE // 2, 1) * sine_left[...] + pltpu.roll(raw, ROPE // 2, 1) * sine_right[...]
    latents[:, rank + KVR :] = jnp.where((lane >= NOPE) & (lane < NOPE + ROPE), turned, 0.0).astype(low)


def down_projections(hidden, pieces, places, chooser, rank, tables):
    rows, width = hidden.shape
    columns = pieces[0].shape[1]
    operands = (hidden, *pieces, chooser, *tables)
    return call(
        functools.partial(down_kernel, rank),
        "down_projections",
        2 * rows * width * columns,
        2 * width * columns,
        grid_spec=pltpu.PrefetchScalarGridSpec(
            num_scalar_prefetch=1,
            grid=(1,),
            in_specs=[whole(*value.shape) for value in operands],
            out_specs=[whole(width, columns), whole(rows, columns), whole(rows, columns), whole(8, width)],
        ),
        out_shape=[shaped((width, columns), low), shaped((rows, columns), wide), shaped((rows, columns), low), shaped((8, width), wide)],
    )(places, *operands)


def feed_kernel(pieces, *refs):
    feeds, (gate_w, upper_w, gate_out, upper_out, inner, feed) = refs[:pieces], refs[pieces:]

    @pl.when(pl.program_id(0) == 0)
    def _():
        join(feed, feeds)

    for begin in range(0, feed.shape[0], 256):
        rows = slice(begin, begin + 256)
        gate = nn(feed[rows], gate_w[...])
        upper = nn(feed[rows], upper_w[...])
        gate_out[rows] = gate.astype(low)
        upper_out[rows] = upper.astype(low)
        inner[rows] = (gate * jax.nn.sigmoid(gate) * upper).astype(low)


def feed_forward(feeds, gate_w, upper_w):
    tokens = sum(p.shape[0] for p in feeds)
    width, hidden_units = gate_w.shape
    size = 256
    column = lambda r: pl.BlockSpec((r, size), lambda i: (0, i))
    return call(
        functools.partial(feed_kernel, len(feeds)),
        "feed_forward",
        4 * tokens * width * hidden_units,
        4 * width * hidden_units,
        grid=(pl.cdiv(hidden_units, size),),
        in_specs=[*[whole(*p.shape) for p in feeds], column(width), column(width)],
        out_specs=[column(tokens), column(tokens), column(tokens), whole(tokens, width)],
        out_shape=[shaped((tokens, hidden_units), low)] * 3 + [shaped((tokens, width), low)],
    )(*feeds, gate_w, upper_w)


def unit_kernel(pieces, places, *refs):
    grads, (gate_in, upper_in, down_w, gate_grad, upper_grad, grad) = refs[:pieces], refs[pieces:]

    @pl.when(pl.program_id(0) == 0)
    def _():
        row = 0
        for piece in grads:
            grad[row : row + piece.shape[0]] = (residual_scale * piece[...].astype(wide)).astype(low)
            row += piece.shape[0]

    for begin in range(0, grad.shape[0], 256):
        rows = slice(begin, begin + 256)
        back = nn(grad[rows], down_w[...])
        gate = gate_in[rows].astype(wide)
        sigmoid = jax.nn.sigmoid(gate)
        gate_grad[rows] = (back * upper_in[rows].astype(wide) * sigmoid * (1.0 + gate * (1.0 - sigmoid))).astype(low)
        upper_grad[rows] = (back * gate * sigmoid).astype(low)


def unit_back(chunk, places, gate, upper, grad_all, down_w):
    tokens, hidden_units = gate.shape
    width = down_w.shape[0]
    size = 256
    column = lambda r: pl.BlockSpec((r, size), lambda i, order: (0, i))
    third, half = tokens // 4, tokens // 8
    near = [pl.BlockSpec((third, width), functools.partial(lambda k, i, order: (order[k] * 2 + chunk, 0), k)) for k in range(3)]
    far = [pl.BlockSpec((half, width), functools.partial(lambda k, i, order: (order[3] * 4 + 2 * chunk + k, 0), k)) for k in range(2)]
    return call(
        functools.partial(unit_kernel, 5),
        "unit_back",
        2 * tokens * width * hidden_units,
        2 * width * hidden_units,
        grid_spec=pltpu.PrefetchScalarGridSpec(
            num_scalar_prefetch=1,
            grid=(pl.cdiv(hidden_units, size),),
            in_specs=[*near, *far, column(tokens), column(tokens), column(width)],
            out_specs=[column(tokens), column(tokens), pl.BlockSpec((tokens, width), lambda i, order: (0, 0))],
        ),
        out_shape=[shaped((tokens, hidden_units), low)] * 2 + [shaped((tokens, width), low)],
    )(places, *[grad_all] * 5, gate, upper, down_w)


def back_kernel(factors, chunks, places, *refs):
    lefts, weights, outs = refs[: factors * chunks], refs[factors * chunks : factors * chunks + factors], refs[factors * chunks + factors :]
    for chunk, out in enumerate(outs):
        found = sum(nt(lefts[f * chunks + chunk][...], weights[f][...]) for f in range(factors)).astype(low)
        rows = out.shape[0] // 4
        for k in range(4):
            out[pl.ds(pl.multiple_of(places[k] * rows, 128), rows)] = found[k * rows : (k + 1) * rows]


def feed_back(name, places, lefts, weights):
    chunks = len(lefts[0])
    flat = [chunk for factor in lefts for chunk in factor]
    tokens, hidden_units = flat[0].shape
    width = weights[0].shape[0]
    size = 256
    return call(
        functools.partial(back_kernel, len(lefts), chunks),
        name,
        2 * len(flat) * tokens * width * hidden_units,
        2 * len(lefts) * width * hidden_units,
        grid_spec=pltpu.PrefetchScalarGridSpec(
            num_scalar_prefetch=1,
            grid=(width // size,),
            in_specs=[*[pl.BlockSpec(p.shape, lambda i, order: (0, 0)) for p in flat], *[pl.BlockSpec((size, hidden_units), lambda i, order: (i, 0))] * len(weights)],
            out_specs=[pl.BlockSpec((tokens, size), lambda i, order: (0, i))] * chunks,
        ),
        out_shape=[shaped((tokens, width), low)] * chunks,
    )(places, *flat, *weights)


def weight_kernel(chunks, groups, *refs):
    lefts = refs[:chunks]
    outs = refs[chunks + chunks * groups :]
    for g, out in enumerate(outs):
        rights = refs[chunks + g * chunks : chunks + (g + 1) * chunks]
        out[...] = sum(tn(left[...], right[...]) for left, right in zip(lefts, rights, strict=True)).astype(low)


def weight_gradients(name, lefts, rights, first=0, width=None):
    chunks, groups = len(lefts), len(rights)
    tokens = lefts[0].shape[0]
    width = width or lefts[0].shape[1]
    columns = rights[0][0].shape[1]
    size = 256
    return call(
        functools.partial(weight_kernel, chunks, groups),
        name,
        2 * groups * chunks * tokens * width * columns,
        2 * (groups * (width + chunks * tokens) * columns + chunks * tokens * width),
        grid=(width // size,),
        in_specs=[*[pl.BlockSpec((tokens, size), lambda i: (0, first // size + i))] * chunks, *[whole(tokens, columns)] * (chunks * groups)],
        out_specs=[pl.BlockSpec((size, columns), lambda i: (i, 0))] * groups,
        out_shape=[shaped((width, columns), low)] * groups,
    )(*lefts, *[r for group in rights for r in group])


def split_cores(core, found, own, other):
    rows = own.shape[1]

    @pl.when(core[0] == 0)
    def _():
        own[0] = found[:rows]
        other[0] = found[rows:]

    @pl.when(core[0] != 0)
    def _():
        own[0] = found[rows:]
        other[0] = found[:rows]


def split_kernel(chunks, core, *refs):
    lefts, rights, outs = refs[:chunks], refs[chunks : 2 * chunks], refs[2 * chunks :]
    split_cores(core, sum(tn(left[...], right[...]) for left, right in zip(lefts, rights, strict=True)).astype(low), *outs)


def split_gradient(name, lefts, rights):
    chunks = len(lefts)
    tokens, width = lefts[0].shape
    columns = rights[0].shape[1]
    size = width // 4
    return call(
        functools.partial(split_kernel, chunks),
        name,
        2 * chunks * tokens * width * columns,
        2 * (width * columns + chunks * tokens * (width + columns)),
        grid_spec=pltpu.PrefetchScalarGridSpec(
            num_scalar_prefetch=1,
            grid=(4,),
            in_specs=[*[pl.BlockSpec((tokens, size), lambda i, core: (0, i))] * chunks, *[pl.BlockSpec((tokens, columns), lambda i, core: (0, 0))] * chunks],
            out_specs=[pl.BlockSpec((1, size // 2, columns), lambda i, core: (i, 0, 0))] * 2,
        ),
        out_shape=[shaped((4, size // 2, columns), low)] * 2,
    )(this_core(), *lefts, *rights)


def latents_kernel(query_grad, expanded_grad, rotary, up_q, up_kv, out):
    rank = up_q.shape[0]
    out[:, :rank] = nt(query_grad[...], up_q[...]).astype(low)
    out[:, rank : rank + KVR] = nt(expanded_grad[...], up_kv[...]).astype(low)
    out[:, rank + KVR :] = rotary[...].astype(low)


def latents_back(query_grad, expanded_grad, rotary, up_q, up_kv):
    group, columns = query_grad.shape
    rank = up_q.shape[0]
    size = 256
    row = lambda w: pl.BlockSpec((size, w), lambda i: (i, 0))
    out_width = rank + KVR + LANES
    return call(
        latents_kernel,
        "latents_back",
        2 * group * columns * (rank + KVR),
        4 * group * columns,
        grid=(group // size,),
        in_specs=[row(columns), row(columns), row(LANES), whole(*up_q.shape), whole(*up_kv.shape)],
        out_specs=row(out_width),
        out_shape=shaped((group, out_width), low),
    )(query_grad, expanded_grad, rotary, up_q, up_kv)


def input_kernel(steps, rank, core, own, one, two, joint, gains, chooser, cosine, sine_left, sine_right, weights, hidden, feed_row, middle_grad, *refs):
    downs_grad, (input_gradient, joint_grad, mixed_row, inverse, total) = refs[:-5], refs[-5:]
    step = pl.program_id(0)
    size, columns = weights.shape
    lanes = pl.ds(pl.multiple_of(step * size, size), size)

    @pl.when(step == 0)
    def _():
        values = hidden[...].astype(wide)
        inverse[...] = jnp.broadcast_to(lax.rsqrt(jnp.mean(values * values, axis=-1, keepdims=True) + epsilon), inverse.shape)
        parts = []
        for begin, end in ((0, rank), (rank, rank + KVR)):
            grad = own[:, begin:end].astype(wide) + one[:, begin:end].astype(wide) + two[:, begin:end].astype(wide)
            part = joint[:, begin:end]
            turn = lax.rsqrt(jnp.mean(part * part, axis=-1, keepdims=True) + epsilon)
            unit = part * turn
            parts.append(jnp.sum(grad * unit, axis=0, keepdims=True))
            joint_grad[:, begin:end] = norm_back(grad, unit, turn, gains[2:3, begin:end]).astype(low)
        lane = lax.broadcasted_iota(jnp.int32, (1, LANES), 1)
        last = slice(rank + KVR, rank + KVR + LANES)
        grad = own[:, last].astype(wide) + one[:, last].astype(wide) + two[:, last].astype(wide)
        back = grad * cosine[...] - pltpu.roll(grad, LANES - ROPE // 2, 1) * sine_left[...] - pltpu.roll(grad, ROPE // 2, 1) * sine_right[...]
        back = jnp.where((lane >= NOPE) & (lane < NOPE + ROPE), back, 0.0)
        joint_grad[:, last] = pltpu.roll(back, LANES - NOPE, 1).astype(low)
        norms = jnp.broadcast_to(jnp.concatenate(parts, axis=1), (8, rank + KVR)).astype(low)
        mixed_row[...] = nt(norms, chooser[...])

    unit = hidden[:, lanes].astype(wide) * inverse[:, :1]
    normed = (unit * gains[0:1, lanes]).astype(low)
    back = nt(joint_grad[...], weights[...])
    total[:, lanes] = back
    found = tn(normed, joint_grad[...])
    gain_row = jnp.sum(back * unit, axis=0, keepdims=True)
    gap = lambda n: jnp.zeros((n, size), wide)
    rows = jnp.concatenate([gap(ROPE), gain_row, feed_row[:, lanes], mixed_row[0:1, lanes], gap(LANES - ROPE - 3)], axis=0)
    found = jnp.concatenate([found[:, : columns - LANES], found[:, columns - LANES :] + rows.T], axis=1).astype(low)
    if len(downs_grad) == 1:
        downs_grad[0][...] = found
    else:
        split_cores(core, found, *downs_grad)

    @pl.when(step == steps - 1)
    def _():
        turn = inverse[:, :1]
        input_gradient[...] = (middle_grad[...] + norm_back(total[...], hidden[...].astype(wide) * turn, turn, gains[0:1])).astype(low)


def input_back(terms, joint, gains, chooser, tables, weights, hidden, feed_row, middle_grad, split):
    rows, width = hidden.shape
    columns = weights.shape[1]
    steps = 4
    size = width // steps
    before = (*terms, joint, gains, chooser, *tables)
    if split:
        out_specs = [pl.BlockSpec((1, size // 2, columns), lambda i, core: (i, 0, 0))] * 2
        out_shape = [shaped((4, size // 2, columns), low)] * 2
    else:
        out_specs = [pl.BlockSpec((size, columns), lambda i, core: (i, 0))]
        out_shape = [shaped((width, columns), low)]
    return call(
        functools.partial(input_kernel, steps, columns - KVR - LANES),
        "input_back",
        4 * rows * width * columns,
        4 * width * columns,
        grid_spec=pltpu.PrefetchScalarGridSpec(
            num_scalar_prefetch=1,
            grid=(steps,),
            in_specs=[*[whole(*p.shape) for p in before], pl.BlockSpec((size, columns), lambda i, core: (i, 0)), whole(rows, width), whole(1, width), whole(rows, width)],
            out_specs=[*out_specs, whole(rows, width)],
            scratch_shapes=[pltpu.VMEM((rows, columns), low), pltpu.VMEM((8, width), wide), pltpu.VMEM((rows, LANES), wide), pltpu.VMEM((rows, width), wide)],
        ),
        out_shape=[*out_shape, shaped((rows, width), low)],
    )(this_core(), *before, weights, hidden, feed_row, middle_grad)


def after(value, *earlier):
    return lax.optimization_barrier((value, *earlier))[0]


def after_all(values, *earlier):
    return list(lax.optimization_barrier((tuple(values), earlier))[0])


def gather_near(block):
    return [block, lax.ppermute(block, "tensor", RIGHT), lax.ppermute(block, "tensor", LEFT)]


def gather_far(near):
    half = near[0].shape[0] // 2
    return [lax.ppermute(near[1][:half], "tensor", RIGHT), lax.ppermute(near[2][half:], "tensor", LEFT)]


def scatter_first(own, to_left, to_right, far_first, far_second):
    half = own.shape[0] // 2
    first = lax.ppermute(far_first, "tensor", LEFT)
    second = lax.ppermute(far_second, "tensor", RIGHT)
    return [jnp.concatenate([to_left[:half] + first, to_left[half:]]), jnp.concatenate([to_right[:half], to_right[half:] + second])]


def scatter_second(sent):
    return [lax.ppermute(sent[0], "tensor", LEFT), lax.ppermute(sent[1], "tensor", RIGHT)]


def add_up(*terms):
    return sum(term.astype(wide) for term in terms)


def exchange_line(blocks):
    own, to_left, to_right, far = blocks
    return [own, lax.ppermute(to_right, "tensor", RIGHT), lax.ppermute(to_left, "tensor", LEFT), lax.ppermute(far, "tensor", OPPOSITE)]


def line_order():
    here = lax.axis_index("tensor")
    return [here, (here + 3) % 4, (here + 1) % 4, (here + 2) % 4]


def this_core():
    return lax.axis_index("dp").astype(jnp.int32)[None] % 2


def flips(bit):
    return [(i, i ^ bit) for i in range(8)]


def cube_near(block):
    return [block, lax.ppermute(block, "dp", flips(2)), lax.ppermute(block, "dp", flips(4))]


def cube_far(near):
    half = near[0].shape[0] // 2
    return [lax.ppermute(near[1][:half], "dp", flips(4)), lax.ppermute(near[2][half:], "dp", flips(2))]


def cube_rows(rows):
    here = lax.axis_index("dp")
    places = [here, here ^ 2, here ^ 4, here ^ 6]
    first = [p * rows for p in (*places, places[3])]
    second = [(p ^ 1) * rows for p in (*places, places[3])]
    first[4] += rows // 2
    second[4] += rows // 2
    return first + second


def swap_cores(blocks):
    return [lax.ppermute(value, "dp", flips(1)) for value in blocks]


def scatter_chips(blocks):
    if blocks.ndim == 2:
        return lax.psum_scatter(blocks, "dp", scatter_dimension=0, tiled=True)
    chips, rows, columns = blocks.shape
    return lax.psum_scatter(blocks.reshape(chips * rows, columns), "dp", scatter_dimension=0, tiled=True, axis_index_groups=[[0, 2, 4, 6], [1, 3, 5, 7]])


def scatter_core(blocks):
    count, rows, columns = blocks.shape
    if count != 8:
        return [blocks]
    core = lax.axis_index("dp") % 2
    other = lax.dynamic_index_in_dim(blocks.reshape(4, 2, rows, columns), 1 - core, 1, keepdims=False)
    return [blocks, lax.ppermute(other, "dp", flips(1))]


def scatter_pair(halves, place):
    here = lax.axis_index("dp")
    pick = lambda array, at: lax.dynamic_index_in_dim(array, at, 0, keepdims=False)
    first = here ^ (2 * place) if halves[0].shape[0] == 8 else (here // 2) ^ place
    return add_up(pick(halves[0], first), pick(halves[1], (here // 2) ^ place))


def mix_kernel(one, two, out):
    out[...] = (one[...].astype(wide) + two[...].astype(wide)).astype(low)


def mix(one, two):
    chips, rows, columns = one.shape
    part = pl.BlockSpec((1, rows, columns), lambda i: (i, 0, 0))
    return call(mix_kernel, "mix", 0, 0, grid=(chips,), in_specs=[part, part], out_specs=part, out_shape=shaped(one.shape, low))(one, two)


def corner_kernel(chip, one, two, first, second):
    half = first.shape[0]
    found = (one[0].astype(wide) + two[0].astype(wide)).astype(low)
    first[...] = found[:half]
    second[...] = found[half:]


def side_kernel(lower, chip, one, two, extra, out):
    half = extra.shape[0]
    found = one[0].astype(wide) + two[0].astype(wide)
    more = extra[...].astype(wide)
    if lower:
        out[:half] = found[:half].astype(low)
        out[half:] = (found[half:] + more).astype(low)
    else:
        out[:half] = (found[:half] + more).astype(low)
        out[half:] = found[half:].astype(low)


def pick_call(kernel, name, halves, place, extras, outs):
    _, rows, columns = halves[0].shape
    chip = (lax.axis_index("dp").astype(jnp.int32) // 2) ^ place
    pick = pl.BlockSpec((1, rows, columns), lambda i, chip: (chip[0], 0, 0))
    fixed = lambda shape: pl.BlockSpec(shape, lambda i, chip: (0, 0))
    spec = pltpu.PrefetchScalarGridSpec(
        num_scalar_prefetch=1,
        grid=(1,),
        in_specs=[pick, pick, *[fixed(e.shape) for e in extras]],
        out_specs=[fixed(shape) for shape in outs],
    )
    return call(kernel, name, 0, 0, grid_spec=spec, out_shape=[shaped(shape, low) for shape in outs])(chip[None], *halves, *extras)


def corner_swap(corner):
    return [lax.ppermute(corner[0], "dp", flips(2)), lax.ppermute(corner[1], "dp", flips(4))]


def corner_sum(halves):
    _, rows, columns = halves[0].shape
    if halves[0].shape[0] == 4:
        return pick_call(corner_kernel, "corner", halves, 3, [], [(rows // 2, columns)] * 2)
    corner = scatter_pair(halves, 3).astype(low)
    return [corner[: rows // 2], corner[rows // 2 :]]


def scatter_corner(halves):
    if len(halves) == 1:
        return halves
    return corner_swap(corner_sum(halves))


def scatter_sides(halves, corners):
    if halves[0].shape[0] == 4:
        shape = halves[0].shape[1:]
        return [
            *pick_call(functools.partial(side_kernel, True), "side", halves, 1, [corners[1]], [shape]),
            *pick_call(functools.partial(side_kernel, False), "side", halves, 2, [corners[0]], [shape]),
        ]
    half = halves[0].shape[1] // 2
    across, along = scatter_pair(halves, 1), scatter_pair(halves, 2)
    across = jnp.concatenate([across[:half], across[half:] + corners[1]]).astype(low)
    along = jnp.concatenate([along[:half] + corners[0], along[half:]]).astype(low)
    return [across, along]


def scatter_swap(sides):
    return [lax.ppermute(sides[0], "dp", flips(2)), lax.ppermute(sides[1], "dp", flips(4))]


def scatter_last(halves, swapped):
    return add_up(scatter_pair(halves, 0), *swapped)


def scatter_rest(halves, corners):
    if len(halves) == 1:
        count, rows, columns = halves[0].shape
        return lax.psum_scatter(corners[0].reshape(count * rows, columns), "dp", scatter_dimension=0, tiled=True).astype(wide)
    return scatter_last(halves, scatter_swap(scatter_sides(halves, corners)))


def local(hidden_in, attention_gain, query_down, query_norm, latent_down, latent_norm, query_up, latent_up, output_weight, feed_gain, gate_weight, up_weight, down_weight, cotangent, document_lengths):
    replicas = lax.axis_size("dp")
    rows, width = hidden_in.shape
    group = rows * 4
    rank = query_down.shape[1]
    heads = query_up.shape[1] // (NOPE + ROPE)
    slice_rows = query_down.shape[0]
    order = line_order()
    joint_width = rank + KVR + LANES
    by_line = lambda array: [lax.dynamic_index_in_dim(array, p, 0, keepdims=False) for p in order]

    def column(value):
        return jnp.pad(value, (0, slice_rows - value.shape[0]))[:, None]

    norms = jnp.concatenate([query_norm, latent_norm])
    downs = jnp.concatenate([query_down, latent_down, column(attention_gain), column(feed_gain), column(norms)], axis=1)
    downs = jnp.pad(downs, ((0, 0), (0, joint_width - downs.shape[1])))
    parts = [slice(k * rows // 2, (k + 1) * rows // 2) for k in range(2)]
    if replicas == 8:
        downs = place(exchange_line([downs] * 4), lambda: [p * slice_rows for p in line_order()], 4 * slice_rows)
    out_near = gather_near(after(output_weight.T, downs))

    query_up_wide = jnp.pad(query_up.reshape(-1, heads, NOPE + ROPE), ((0, 0), (0, 0), (0, LANES - NOPE - ROPE))).reshape(-1, heads * LANES)
    ups_all = lax.all_gather(jnp.concatenate([query_up_wide, latent_up], axis=0), "dp", axis=0)
    up_q = ups_all[:, : query_up.shape[0]].reshape(rank, heads * LANES)
    up_kv = ups_all[:, query_up.shape[0] :].reshape(KVR, heads * LANES)

    grad_all = lax.all_gather(cotangent, "tensor", axis=0, tiled=True)
    segment, position = layout(document_lengths[0], group)
    cosine_half, sine_half = rotary_tables(position, ROPE)
    zeros = lambda n: jnp.zeros((group, n), wide)
    cosine_wide = jnp.concatenate([jnp.ones((group, NOPE), wide), cosine_half, cosine_half, zeros(ROPE)], axis=1)
    sine_left = jnp.concatenate([zeros(NOPE), -sine_half, zeros(ROPE // 2 + ROPE)], axis=1)
    sine_right = jnp.concatenate([zeros(NOPE + ROPE // 2), sine_half, zeros(ROPE)], axis=1)
    segment_col, segment_row = segment[:, None], segment[None, :]
    first_row = lax.axis_index("tensor") * rows
    local_tables = [lax.dynamic_slice_in_dim(t, first_row, rows, 0) for t in (cosine_wide, sine_left, sine_right)]
    a, b = query_norm.shape[0], norms.shape[0]
    lanes = jnp.arange(rank + KVR)
    source = jnp.where(lanes < rank, lanes // a * slice_rows + lanes % a, (lanes - rank) // (b - a) * slice_rows + a + (lanes - rank) % (b - a))
    chooser = (jnp.arange(width)[:, None] == source[None, :]).astype(low)
    ready = (chooser, cosine_wide, sine_left, sine_right, segment_col, *local_tables)
    if replicas == 8:
        near = after_all(cube_near(downs), *out_near)
        out_far = gather_far(after_all(out_near, near[1]))
        near = after_all(near + cube_far(near), *out_far)
        down_pieces = after_all(near + swap_cores(near), *ready)
        down_places = jnp.stack(cube_rows(near[0].shape[0])).astype(jnp.int32)
    else:
        down_pieces = [lax.all_gather(downs, ("dp", "tensor"), axis=0, tiled=True)]
        down_places = jnp.zeros((1,), jnp.int32)
        out_far = gather_far(out_near)
    gate_all = lax.all_gather(after(gate_weight, down_pieces[0]), "dp", axis=0, tiled=True)
    weights_down, joint, latents_own, gains = down_projections(hidden_in, down_pieces, down_places, chooser, rank, local_tables)
    feed_scale = gains[1:2]
    latents_near = gather_near(latents_own)
    latents_near = after_all(latents_near, up_q, up_kv)

    out_block = after(jnp.concatenate([*out_near, jnp.concatenate(out_far, axis=0)], axis=1), down_pieces[0])
    if replicas == 8:
        out_blocks = cube_near(out_block)
        latents_near = after_all(latents_near, *out_blocks)
        out_blocks += cube_far(out_blocks)
        out_soon = out_blocks
    else:
        out_all = lax.all_gather(out_block, "dp", axis=0, tiled=True)
        out_soon = [out_all]
    latents_far = gather_far(latents_near)

    def latent_rows():
        here = line_order()
        return [here[0] * rows, here[1] * rows, here[2] * rows, here[3] * rows, here[3] * rows + rows // 2]

    latents = place(after_all(latents_near + latents_far, *out_soon), latent_rows, group)
    upper_all = lax.all_gather(after(up_weight, latents), "dp", axis=0, tiled=True)
    down_all = lax.all_gather(after(down_weight.T, latents), "dp", axis=0, tiled=True)

    block = min(256, group)
    pairs = heads // 2
    by_pair = lambda r, w: pl.BlockSpec((r, w), lambda i: (0, i))
    attended, queries, expanded, log_total = call(
        functools.partial(attention_forward_kernel, rank, block),
        "attention_forward",
        20 * 10**9,
        15 * 10**6,
        grid=(pairs,),
        in_specs=[whole(group, joint_width), by_pair(rank, 2 * LANES), by_pair(KVR, 2 * LANES), whole(group, LANES), whole(group, LANES), whole(group, LANES), whole(group, 1), whole(1, group)],
        out_specs=[by_pair(group, LANES), by_pair(group, 2 * LANES), by_pair(group, 2 * LANES), whole(group, LANES)],
        out_shape=[shaped((group, heads * VD), low), shaped((group, heads * LANES), low), shaped((group, heads * LANES), low), shaped((group, LANES), wide)],
    )(latents, up_q, up_kv, cosine_wide, sine_left, sine_right, segment_col, segment_row)
    log_rows = log_total[:, :16].T

    if replicas == 8:
        out_other = after_all(swap_cores(out_blocks), attended)
        out_all = place(out_blocks + out_other, lambda: cube_rows(out_block.shape[0]), 8 * out_block.shape[0])

    attended_parts = lax.all_to_all(attended.reshape(4, rows, heads * VD), "tensor", 0, 0)
    attended_own = jnp.concatenate(by_line(attended_parts), axis=1)
    attended_own = after(attended_own, grad_all)
    middle = hidden_in.astype(wide) + residual_scale * nt(attended_own, out_all)
    inverse_middle = inverse_rms(middle)
    unit_middle = middle * inverse_middle
    feed_in = (unit_middle * feed_scale).astype(low)

    near_0 = gather_near(feed_in[parts[0]])
    far_0 = gather_far(near_0)
    near_1 = gather_near(after(feed_in[parts[1]], *far_0))
    places = jnp.stack(order).astype(jnp.int32)
    gate, upper, inner_0, feed_0 = feed_forward(near_0 + far_0, gate_all, upper_all)
    far_1 = gather_far(after_all(near_1, inner_0))
    gate_0, upper_0, grad_0 = unit_back(0, places, *after_all([gate, upper], *far_1), grad_all, down_all)
    (part_0,) = feed_back("feed_back", places, [[gate_0], [upper_0]], [gate_all, upper_all])
    gate, upper, inner_1, feed_1 = feed_forward(after_all(near_1 + far_1, part_0), gate_all, upper_all)
    gate_1, upper_1, grad_1 = unit_back(1, places, gate, upper, grad_all, down_all)
    (part_1,) = feed_back("feed_back", places, [[gate_1], [upper_1]], [gate_all, upper_all])
    down_lefts = after_all([grad_0, grad_1], part_1)
    if replicas == 8:
        down_own, down_grad = split_gradient("down_gradient", down_lefts, [inner_0, inner_1])
        down_core = [down_own, *swap_cores([down_grad])]
    else:
        (down_grad,) = weight_gradients("down_gradient", down_lefts, [[inner_0, inner_1]])
        down_core = scatter_core(down_grad.reshape(replicas, -1, down_grad.shape[1]))
    gate_lefts = after_all([feed_0, feed_1], down_grad)
    if replicas == 8:
        gate_own, gate_grad = split_gradient("gate_gradient", gate_lefts, [gate_0, gate_1])
        upper_own, upper_grad = split_gradient("upper_gradient", after_all(gate_lefts, gate_grad), [upper_0, upper_1])
        gate_chips = mix(gate_own, *swap_cores([gate_grad]))
        upper_chips = mix(upper_own, *swap_cores([upper_grad]))
    else:
        gate_grad, upper_grad = weight_gradients("gate_gradient", gate_lefts, [[gate_0, gate_1], [upper_0, upper_1]])
        gate_chips, upper_chips = gate_grad, upper_grad
    got_0 = lax.psum_scatter(part_0, "tensor", scatter_dimension=0, tiled=True)
    got_1 = lax.psum_scatter(part_1, "tensor", scatter_dimension=0, tiled=True)
    down_mixed = corner_sum(down_core) if replicas == 8 else down_core
    down_corner = corner_swap(down_mixed) if replicas == 8 else down_core
    down_sides = scatter_sides(down_core, down_corner) if replicas == 8 else down_corner
    gate_sum = scatter_chips(gate_chips)
    got_0, got_1 = after_all([got_0, got_1], gate_chips, upper_chips, *down_mixed)
    feed_in_grad = jnp.concatenate([got_0, got_1]).astype(wide)

    feed_gain_part = jnp.sum(feed_in_grad * unit_middle, axis=0, keepdims=True)
    middle_grad = cotangent.astype(wide) + norm_back(feed_in_grad, unit_middle, inverse_middle, feed_scale)
    branch_one_grad = (residual_scale * middle_grad).astype(low)
    attended_grad_own = nn(branch_one_grad, out_all).astype(low)
    attended_grads = jnp.zeros((4, rows, heads * VD), low)
    for k, p in enumerate(order):
        attended_grads = lax.dynamic_update_index_in_dim(attended_grads, attended_grad_own[:, k * heads * VD : (k + 1) * heads * VD], p, 0)
    out_left = after(branch_one_grad, attended_grad_own)
    if replicas == 8:
        out_own, out_grad = split_gradient("out_gradient", [out_left], [attended_own])
        out_core = [out_own, *swap_cores([out_grad])]
    else:
        out_grad = tn(out_left, attended_own).astype(low)
        out_core = scatter_core(out_grad.reshape(replicas, -1, 4 * heads * VD))
    attended_grad = lax.all_to_all(after(attended_grads, out_grad), "tensor", 0, 0).reshape(group, heads * VD)
    outs = feed_back("branch_two", places, [after_all([inner_0, inner_1], attended_grad_own)], [down_all])
    attended_grad = after(attended_grad, *outs, *out_core)
    branch_two = [lax.psum_scatter(after(outs[0], attended_grad), "tensor", scatter_dimension=0, tiled=True)]
    upper_sum = scatter_chips(after(upper_chips, attended_grad))
    out_corner = scatter_corner(out_core)
    down_swapped = scatter_swap(down_sides) if replicas == 8 else down_corner

    query_grad, expanded_grad, rotary_grad = call(
        functools.partial(attention_backward_kernel, block),
        "attention_backward",
        30 * 10**9,
        15 * 10**6,
        grid=(pairs,),
        in_specs=[by_pair(group, 2 * LANES), by_pair(group, 2 * LANES), pl.BlockSpec((group, LANES), lambda i: (0, (rank + KVR) // LANES)), whole(group, LANES), whole(group, LANES), whole(group, LANES), whole(group, 1), whole(1, group), whole(16, group), by_pair(group, LANES)],
        out_specs=[by_pair(group, 2 * LANES), by_pair(group, 2 * LANES), whole(group, LANES)],
        out_shape=[shaped((group, heads * LANES), low), shaped((group, heads * LANES), low), shaped((group, LANES), wide)],
        scratch_shapes=[pltpu.VMEM((group, LANES), wide), pltpu.VMEM((group, LANES), wide)],
    )(queries, expanded, latents, cosine_wide, sine_left, sine_right, segment_col, segment_row, log_rows, attended_grad)

    latents_part = latents_back(*after_all([query_grad, expanded_grad, rotary_grad], *down_swapped, *out_corner), up_q, up_kv)
    cut = by_line(latents_part.reshape(4, rows, joint_width))
    sent = scatter_first(*cut[:3], cut[3][: rows // 2], cut[3][rows // 2 :])

    turn = after(latents, *sent)
    (query_up_grad,) = weight_gradients("query_up_gradient", [turn], [[query_grad]], 0, rank)
    (latent_up_grad,) = weight_gradients("latent_up_gradient", [turn], [[expanded_grad]], rank, KVR)
    ups_grad = jnp.concatenate([query_up_grad.reshape(replicas, -1, heads * LANES), latent_up_grad.reshape(replicas, -1, heads * LANES)], axis=1)
    ups_core = scatter_core(ups_grad)
    out_swapped = scatter_swap(scatter_sides(after_all(out_core, cut[0]), out_corner)) if replicas == 8 else out_corner
    latents_terms = after_all([cut[0], *scatter_second(sent)], *ups_core, *out_swapped, *outs)
    branch_two.append(lax.psum_scatter(after(outs[1], *latents_terms), "tensor", scatter_dimension=0, tiled=True))
    ups_corner = scatter_corner(ups_core)
    *downs_grad, input_gradient = input_back(latents_terms, joint, gains, chooser, local_tables, weights_down, hidden_in, feed_gain_part, middle_grad, replicas == 8)
    downs_grad = after_all(downs_grad, *ups_corner)
    if replicas == 8:
        downs_core = [downs_grad[0], *swap_cores(downs_grad[1:])]
        downs_part = scatter_rest(downs_core, scatter_corner(downs_core)).astype(low).reshape(4, slice_rows, joint_width)
        downs_sum = sum(p.astype(wide) for p in exchange_line(by_line(downs_part)))
        out_part = scatter_last(out_core, out_swapped).astype(low)
    else:
        downs_sum = lax.psum_scatter(downs_grad[0], ("dp", "tensor"), scatter_dimension=0, tiled=True).astype(wide)
        out_part = scatter_rest(out_core, out_corner).astype(low)
    out_got = exchange_line([out_part[:, k * heads * VD : (k + 1) * heads * VD] for k in range(4)])
    ups_sum = scatter_rest(ups_core, ups_corner)
    gain_sums = downs_sum[:, rank + KVR + ROPE : rank + KVR + ROPE + 3].T

    output_sum = add_up(*out_got).T

    gate_sum, upper_sum, *branch_two = [v.astype(wide) for v in after_all([gate_sum, upper_sum, *branch_two], downs_sum)]
    layer_output = (middle + residual_scale * jnp.concatenate(branch_two)).astype(low)
    if replicas == 8:
        down_sum = scatter_last(after_all(down_core, *downs_grad), down_swapped).T
    else:
        down_sum = scatter_rest(down_core, down_corner).T
    query_up_sum = ups_sum[: query_up.shape[0]].reshape(-1, heads, LANES)[..., : NOPE + ROPE].reshape(query_up.shape)
    return (
        layer_output,
        input_gradient,
        gain_sums[0],
        downs_sum[:, :rank],
        gain_sums[2, :a],
        downs_sum[:, rank : rank + KVR + ROPE],
        gain_sums[2, a:b],
        query_up_sum,
        ups_sum[query_up.shape[0] :],
        output_sum,
        gain_sums[1],
        gate_sum,
        upper_sum,
        down_sum,
    )


def solution(mesh):
    return jax.shard_map(
        local,
        mesh=mesh,
        in_specs=(
            P(("dp", "tensor"), None),
            P(("dp", "tensor")),
            P(("dp", "tensor"), None),
            P(("dp", "tensor")),
            P(("dp", "tensor"), None),
            P(("dp", "tensor")),
            P("dp", "tensor"),
            P("dp", "tensor"),
            P("tensor", "dp"),
            P(("dp", "tensor")),
            P("dp", "tensor"),
            P("dp", "tensor"),
            P("tensor", "dp"),
            P(("dp", "tensor"), None),
            P("dp", None),
        ),
        out_specs=(
            P(("dp", "tensor"), None),
            P(("dp", "tensor"), None),
            P(("dp", "tensor")),
            P(("dp", "tensor"), None),
            P(("dp", "tensor")),
            P(("dp", "tensor"), None),
            P(("dp", "tensor")),
            P("dp", "tensor"),
            P("dp", "tensor"),
            P("tensor", "dp"),
            P(("dp", "tensor")),
            P("dp", "tensor"),
            P("dp", "tensor"),
            P("tensor", "dp"),
        ),
        check_vma=False,
    )
```

profile of v0, /device:TPU:0, one launch (start us, length us, event | category | flops | bytes accessed | tf_op | source)
XLA Modules:
  0.0 853.0 jit_solution(10869880718537549246)
XLA Ops:
  45.9 11.7 %collective-permute-done.5 = bf16[320,640]{1,0:T(8,128)(2,1)S(1)} collective-permute-done((bf16[320,640]{1,0:T(8,128)(2,1)S(1)}, bf16[320,640]{1,0:T(8,128)(2,1)S(1)}, u32[]{:S(2)}, u32[]{:S(2)}) %collective-permute-start.5) | collective-permute-done | bytes 409632 | tf_op jit(solution)/shard_map/ppermute | solution.py:526
  65.5 19.9 %collective-permute-done.10 = bf16[160,640]{1,0:T(8,128)(2,1)S(1)} collective-permute-done((bf16[160,640]{1,0:T(8,128)(2,1)S(1)}, bf16[160,640]{1,0:T(8,128)(2,1)S(1)}, u32[]{:S(2)}, u32[]{:S(2)}) %collective-permute-start.10) | collective-permute-done | bytes 204832 | tf_op jit(solution)/shard_map/ppermute | solution.py:531
  95.1 10.3 %down_projections.1 = (bf16[2560,1152]{1,0:T(8,128)(2,1)}, f32[256,1152]{1,0:T(8,128)}, bf16[256,1152]{1,0:T(8,128)(2,1)}, f32[8,2560]{1,0:T(8,128)}) custom-call(s32[10]{0:T(128)} %stack.58.places, bf16[256,2560]{1,0:T(8,128)(2,1)} %hidden.3, bf16[320,1152]{1,0:T(8,128)(2,1)} %place.3.refs_0_, bf16[320,1152]{1,0:T(8,128)(2,1)} %collective-permute-done.3.refs_1_, ...), custom_call_target="tpu_custom_call" | custom-call | tf_op jit(solution)/shard_map/down_projections/pallas_call | solution.py:232
  107.7 23.9 %collective-permute-done.19.refs_2_ = bf16[320,2560]{1,0:T(8,128)(2,1)} collective-permute-done((bf16[320,2560]{1,0:T(8,128)(2,1)S(1)}, bf16[320,2560]{1,0:T(8,128)(2,1)}, u32[]{:S(2)}, u32[]{:S(2)}) %collective-permute-start.19) | collective-permute-done | bytes 1638432 | tf_op jit(solution)/shard_map/ppermute | solution.py:568
  141.4 18.7 %collective-permute-done.17.refs_2_ = bf16[256,1152]{1,0:T(8,128)(2,1)} collective-permute-done((bf16[256,1152]{1,0:T(8,128)(2,1)}, bf16[256,1152]{1,0:T(8,128)(2,1)}, u32[]{:S(2)}, u32[]{:S(2)}) %collective-permute-start.17) | collective-permute-done | bytes 589856 | tf_op jit(solution)/shard_map/ppermute | solution.py:526
  165.9 18.5 %collective-permute-done.21.refs_4_ = bf16[128,1152]{1,0:T(8,128)(2,1)S(1)} collective-permute-done((bf16[128,1152]{1,0:T(8,128)(2,1)S(1)}, bf16[128,1152]{1,0:T(8,128)(2,1)S(1)}, u32[]{:S(2)}, u32[]{:S(2)}) %collective-permute-start.21) | collective-permute-done | bytes 294944 | tf_op jit(solution)/shard_map/ppermute | solution.py:531
  197.7 30.9 %attention_forward.1 = (bf16[1024,640]{1,0:T(8,128)(2,1)}, bf16[1024,1280]{1,0:T(8,128)(2,1)}, bf16[1024,1280]{1,0:T(8,128)(2,1)}, f32[1024,128]{1,0:T(8,128)}) custom-call(bf16[1024,1152]{1,0:T(8,128)(2,1)} %place.4.latents.rotary_in.refs_0_, bf16[768,1280]{1,0:T(8,128)(2,1)} %bitcast.155, bf16[256,1280]{1,0:T(8,128)(2,1)} %bitcast.167, ...), custom_call_target="tpu_custom_call" | custom-call | tf_op jit(solution)/shard_map/attention_forward/pallas_call | solution.py:783
  244.9 9.2 %place.5 = bf16[2560,2560]{1,0:T(8,128)(2,1)} custom-call(bf16[320,2560]{1,0:T(8,128)(2,1)} %copy-done.3, bf16[320,2560]{1,0:T(8,128)(2,1)} %copy-done.10, bf16[320,2560]{1,0:T(8,128)(2,1)} %collective-permute-done.19.refs_2_, bf16[160,2560]{1,0:T(8,128)(2,1)} %collective-permute-done.22.refs_3_, bf16[160,2560]{1,0:T(8,128)(2,1)} %collective-permute-done.23.refs_4_, ...), custom_call_target="tpu_custom_call" | custom-call | tf_op jit(solution)/shard_map/place/pallas_call | solution.py:187
  254.1 9.2 %all-to-all-done = bf16[4,256,640]{2,1,0:T(8,128)(2,1)S(1)} async-done(((bf16[4,256,640]{2,1,0:T(8,128)(2,1)}), bf16[4,256,640]{2,1,0:T(8,128)(2,1)S(1)}, u32[]{:S(2)}, u32[]{:S(2)}) %all-to-all-start) | async-done | bytes 1310752 | tf_op jit(solution)/shard_map/all_to_all | solution.py:799
  264.6 9.2 %multiply_reduce_fusion = (f32[256]{0:T(256)S(1)}, f32[256,2560]{1,0:T(8,128)S(1)}) fusion(bf16[256,2560]{1,0:T(8,128)(2,1)} %pad_maximum_fusion.1.refs_1_, bf16[2560,2560]{1,0:T(8,128)(2,1)} %place.5, bf16[256,2560]{1,0:T(8,128)(2,1)} %hidden.3), kind=kOutput, calls=%fused_computation.30 | convolution fusion | flops 3358719744 | bytes 18351104 | tf_op jit(solution)/shard_map/dot_general | solution.py:15
  276.2 27.6 %collective-permute-done.30.refs_2_ = bf16[128,2560]{1,0:T(8,128)(2,1)S(1)} collective-permute-done((bf16[128,2560]{1,0:T(8,128)(2,1)S(1)}, bf16[128,2560]{1,0:T(8,128)(2,1)S(1)}, u32[]{:S(2)}, u32[]{:S(2)}) %collective-permute-start.30) | collective-permute-done | bytes 655392 | tf_op jit(solution)/shard_map/ppermute | solution.py:526
  307.4 10.6 %collective-permute-done.32.refs_4_ = bf16[64,2560]{1,0:T(8,128)(2,1)S(1)} collective-permute-done((bf16[64,2560]{1,0:T(8,128)(2,1)S(1)}, bf16[64,2560]{1,0:T(8,128)(2,1)S(1)}, u32[]{:S(2)}, u32[]{:S(2)}) %collective-permute-start.32) | collective-permute-done | bytes 327712 | tf_op jit(solution)/shard_map/ppermute | solution.py:531
  320.6 16.3 %feed_forward.2 = (bf16[512,1600]{1,0:T(8,128)(2,1)}, bf16[512,1600]{1,0:T(8,128)(2,1)}, bf16[512,1600]{1,0:T(8,128)(2,1)}, bf16[512,2560]{1,0:T(8,128)(2,1)}) custom-call(bf16[128,2560]{1,0:T(8,128)(2,1)} %copy-done.14, bf16[128,2560]{1,0:T(8,128)(2,1)} %copy-done.20, bf16[128,2560]{1,0:T(8,128)(2,1)} %copy-done.19, bf16[64,2560]{1,0:T(8,128)(2,1)} %copy-done.36, ...), custom_call_target="tpu_custom_call" | custom-call | tf_op jit(solution)/shard_map/feed_forward/pallas_call | solution.py:268
  337.0 12.5 %collective-permute-done.33.refs_1_ = bf16[128,2560]{1,0:T(8,128)(2,1)} collective-permute-done((bf16[128,2560]{1,0:T(8,128)(2,1)S(1)}, bf16[128,2560]{1,0:T(8,128)(2,1)}, u32[]{:S(2)}, u32[]{:S(2)}) %collective-permute-start.33) | collective-permute-done | bytes 655392 | tf_op jit(solution)/shard_map/ppermute | solution.py:526
  367.9 13.7 %unit_back.2 = (bf16[512,1600]{1,0:T(8,128)(2,1)}, bf16[512,1600]{1,0:T(8,128)(2,1)}, bf16[512,2560]{1,0:T(8,128)(2,1)}) custom-call(s32[4]{0:T(128)} %pad_add_fusion.1.places, bf16[1024,2560]{1,0:T(8,128)(2,1)} %all-gather.7.cloned.1.call-done.refs_0_.refs_1_.refs_2_.refs_3_.refs_4_, ...), custom_call_target="tpu_custom_call" | custom-call | tf_op jit(solution)/shard_map/unit_back/pallas_call | solution.py:307
  381.6 17.1 %feed_back.2 = bf16[512,2560]{1,0:T(8,128)(2,1)} custom-call(s32[4]{0:T(128)} %pad_add_fusion.1.places, bf16[512,1600]{1,0:T(8,128)(2,1)} %get-tuple-element.197.refs_0_.refs_2_, bf16[512,1600]{1,0:T(8,128)(2,1)} %get-tuple-element.198.refs_1_.refs_2_, bf16[2560,1600]{1,0:T(8,128)(2,1)} %all-gather.9.cloned.1.call-done.refs_5_.refs_2_, ...), custom_call_target="tpu_custom_call" | custom-call | tf_op jit(solution)/shard_map/feed_back/pallas_call | solution.py:337
  398.8 16.7 %feed_forward.3 = (bf16[512,1600]{1,0:T(8,128)(2,1)}, bf16[512,1600]{1,0:T(8,128)(2,1)}, bf16[512,1600]{1,0:T(8,128)(2,1)}, bf16[512,2560]{1,0:T(8,128)(2,1)}) custom-call(bf16[128,2560]{1,0:T(8,128)(2,1)} %copy-done.13, bf16[128,2560]{1,0:T(8,128)(2,1)} %collective-permute-done.33.refs_1_, bf16[128,2560]{1,0:T(8,128)(2,1)} %collective-permute-done.34.refs_2_, ...), custom_call_target="tpu_custom_call" | custom-call | tf_op jit(solution)/shard_map/feed_forward/pallas_call | solution.py:268
  415.5 13.9 %unit_back.3 = (bf16[512,1600]{1,0:T(8,128)(2,1)}, bf16[512,1600]{1,0:T(8,128)(2,1)}, bf16[512,2560]{1,0:T(8,128)(2,1)}) custom-call(s32[4]{0:T(128)} %pad_add_fusion.1.places, bf16[1024,2560]{1,0:T(8,128)(2,1)} %all-gather.7.cloned.1.call-done.refs_0_.refs_1_.refs_2_.refs_3_.refs_4_, ...), custom_call_target="tpu_custom_call" | custom-call | tf_op jit(solution)/shard_map/unit_back/pallas_call | solution.py:307
  429.4 17.1 %feed_back.3 = bf16[512,2560]{1,0:T(8,128)(2,1)} custom-call(s32[4]{0:T(128)} %pad_add_fusion.1.places, bf16[512,1600]{1,0:T(8,128)(2,1)} %get-tuple-element.209.refs_0_.refs_3_, bf16[512,1600]{1,0:T(8,128)(2,1)} %get-tuple-element.210.refs_1_.refs_3_, bf16[2560,1600]{1,0:T(8,128)(2,1)} %all-gather.9.cloned.1.call-done.refs_5_.refs_2_, ...), custom_call_target="tpu_custom_call" | custom-call | tf_op jit(solution)/shard_map/feed_back/pallas_call | solution.py:337
  447.0 15.0 %down_gradient.1 = (bf16[4,320,1600]{2,1,0:T(8,128)(2,1)}, bf16[4,320,1600]{2,1,0:T(8,128)(2,1)}) custom-call(s32[1]{0:T(128)S(6)} %select_n.206.core, bf16[512,2560]{1,0:T(8,128)(2,1)} %get-tuple-element.211.refs_0_, bf16[512,2560]{1,0:T(8,128)(2,1)} %get-tuple-element.212.refs_1_, bf16[512,1600]{1,0:T(8,128)(2,1)} %get-tuple-element.231.refs_2_.refs_0_, ...), custom_call_target="tpu_custom_call" | custom-call | tf_op jit(solution)/shard_map/down_gradient/pallas_call | solution.py:402
  462.0 15.0 %gate_gradient.1 = (bf16[4,320,1600]{2,1,0:T(8,128)(2,1)}, bf16[4,320,1600]{2,1,0:T(8,128)(2,1)}) custom-call(s32[1]{0:T(128)S(6)} %select_n.206.core, bf16[512,2560]{1,0:T(8,128)(2,1)} %get-tuple-element.219.refs_0_, bf16[512,2560]{1,0:T(8,128)(2,1)} %get-tuple-element.220.refs_1_, bf16[512,1600]{1,0:T(8,128)(2,1)} %get-tuple-element.197.refs_0_.refs_2_, ...), custom_call_target="tpu_custom_call" | custom-call | tf_op jit(solution)/shard_map/gate_gradient/pallas_call | solution.py:402
  477.0 15.1 %upper_gradient.1 = (bf16[4,320,1600]{2,1,0:T(8,128)(2,1)}, bf16[4,320,1600]{2,1,0:T(8,128)(2,1)}) custom-call(s32[1]{0:T(128)S(6)} %select_n.206.core, bf16[512,2560]{1,0:T(8,128)(2,1)} %get-tuple-element.219.refs_0_, bf16[512,2560]{1,0:T(8,128)(2,1)} %get-tuple-element.220.refs_1_, bf16[512,1600]{1,0:T(8,128)(2,1)} %get-tuple-element.198.refs_1_.refs_2_, ...), custom_call_target="tpu_custom_call" | custom-call | tf_op jit(solution)/shard_map/upper_gradient/pallas_call | solution.py:402
  522.5 9.3 %out_gradient.1 = (bf16[4,320,2560]{2,1,0:T(8,128)(2,1)}, bf16[4,320,2560]{2,1,0:T(8,128)(2,1)}) custom-call(s32[1]{0:T(128)S(6)} %select_n.206.core, bf16[256,2560]{1,0:T(8,128)(2,1)} %copy-done.9, bf16[256,2560]{1,0:T(8,128)(2,1)} %pad_maximum_fusion.1.refs_1_), custom_call_target="tpu_custom_call" | custom-call | tf_op jit(solution)/shard_map/out_gradient/pallas_call | solution.py:402
  540.6 16.4 %branch_two.1 = (bf16[512,2560]{1,0:T(8,128)(2,1)}, bf16[512,2560]{1,0:T(8,128)(2,1)}) custom-call(s32[4]{0:T(128)} %pad_add_fusion.1.places, bf16[512,1600]{1,0:T(8,128)(2,1)} %get-tuple-element.231.refs_2_.refs_0_, bf16[512,1600]{1,0:T(8,128)(2,1)} %get-tuple-element.232.refs_3_.refs_1_, bf16[2560,1600]{1,0:T(8,128)(2,1)} %all-gather.13.cloned.1.call-done.refs_7_.refs_2_), custom_call_target="tpu_custom_call" | custom-call | tf_op jit(solution)/shard_map/branch_two/pallas_call | solution.py:337
  557.0 15.7 %all-to-all-done.1 = bf16[4,256,640]{2,1,0:T(8,128)(2,1)} async-done(((bf16[4,256,640]{2,1,0:T(8,128)(2,1)}), bf16[4,256,640]{2,1,0:T(8,128)(2,1)}, u32[]{:S(2)}, u32[]{:S(2)}) %all-to-all-start.1) | async-done | bytes 1310752 | tf_op jit(solution)/shard_map/all_to_all | solution.py:857
  574.8 11.9 %collective-permute-done.41.extra = bf16[160,1600]{1,0:T(8,128)(2,1)} collective-permute-done((bf16[160,1600]{1,0:T(8,128)(2,1)}, bf16[160,1600]{1,0:T(8,128)(2,1)}, u32[]{:S(2)}, u32[]{:S(2)}) %collective-permute-start.41) | collective-permute-done | bytes 512032 | tf_op jit(solution)/shard_map/ppermute | solution.py:657
  604.3 31.4 %attention_backward.1 = (bf16[1024,1280]{1,0:T(8,128)(2,1)}, bf16[1024,1280]{1,0:T(8,128)(2,1)}, f32[1024,128]{1,0:T(8,128)}) custom-call(bf16[1024,1280]{1,0:T(8,128)(2,1)} %get-tuple-element.239.queries, bf16[1024,1280]{1,0:T(8,128)(2,1)} %get-tuple-element.240.expanded, bf16[1024,1152]{1,0:T(8,128)(2,1)} %place.4.latents.rotary_in.refs_0_, ...), custom_call_target="tpu_custom_call" | custom-call | tf_op jit(solution)/shard_map/attention_backward/pallas_call | solution.py:865
  675.6 13.7 %collective-permute-done.48.one = bf16[256,1152]{1,0:T(8,128)(2,1)S(1)} collective-permute-done((bf16[256,1152]{1,0:T(8,128)(2,1)S(1)}, bf16[256,1152]{1,0:T(8,128)(2,1)S(1)}, u32[]{:S(2)}, u32[]{:S(2)}) %collective-permute-start.48) | collective-permute-done | bytes 589856 | tf_op jit(solution)/shard_map/ppermute | solution.py:542
  689.3 12.9 %collective-permute-done.50.two = bf16[256,1152]{1,0:T(8,128)(2,1)S(1)} collective-permute-done((bf16[256,1152]{1,0:T(8,128)(2,1)S(1)}, bf16[256,1152]{1,0:T(8,128)(2,1)S(1)}, u32[]{:S(2)}, u32[]{:S(2)}) %collective-permute-start.50) | collective-permute-done | bytes 589856 | tf_op jit(solution)/shard_map/ppermute | solution.py:542
  710.0 15.9 %input_back.1 = (bf16[4,320,1152]{2,1,0:T(8,128)(2,1)}, bf16[4,320,1152]{2,1,0:T(8,128)(2,1)}, bf16[256,2560]{1,0:T(8,128)(2,1)}) custom-call(s32[1]{0:T(128)S(6)} %select_n.206.core, bf16[256,1152]{1,0:T(8,128)(2,1)} %dynamic-slice_bitcast_fusion.own, bf16[256,1152]{1,0:T(8,128)(2,1)} %copy-done.27, bf16[256,1152]{1,0:T(8,128)(2,1)} %copy-done.28, ...), custom_call_target="tpu_custom_call" | custom-call | tf_op jit(solution)/shard_map/input_back/pallas_call | solution.py:501
  768.0 11.3 %collective-permute-done.68 = bf16[320,640]{1,0:T(8,128)(2,1)} collective-permute-done((bf16[320,640]{1,0:T(8,128)(2,1)}, bf16[320,640]{1,0:T(8,128)(2,1)}, u32[]{:S(2)}, u32[]{:S(2)}) %collective-permute-start.68) | collective-permute-done | bytes 409632 | tf_op jit(solution)/shard_map/ppermute | solution.py:551
  813.8 26.2 %reduce-scatter.13.cloned.1.call-done = bf16[320,1600]{1,0:T(8,128)(2,1)} async-done(((bf16[1280,1600]{1,0:T(8,128)(2,1)}), bf16[320,1600]{1,0:T(8,128)(2,1)}) %reduce-scatter.13.cloned.1.call-update) | async-done | bytes 1024016 | tf_op jit(solution)/shard_map/reduce_scatter | solution.py:594
  (384 shorter events, 321.0 us)
Async XLA Ops:
  7.2 128.9 %all-gather.15.cloned.1.call-start = ((), (), s32[]{:S(2)}) async-start(), calls=%async_computation.18 | async-start | bytes 2949120 | tf_op jit(solution)/shard_map/all_gather | solution.py:726
  10.6 254.0 %all-gather.7.cloned.1.call-start = ((), (), s32[]{:S(2)}) async-start(), calls=%async_computation.8 | async-start | bytes 6553600 | tf_op jit(solution)/shard_map/all_gather | solution.py:730
  11.3 309.3 %all-gather.9.cloned.1.call-start = ((), (), s32[]{:S(2)}) async-start(), calls=%async_computation.9 | async-start | bytes 9584640 | tf_op jit(solution)/shard_map/all_gather | solution.py:755
  91.6 229.0 %all-gather.11.cloned.1.call-start = ((), (), s32[]{:S(2)}) async-start(), calls=%async_computation.10 | async-start | bytes 9584640 | tf_op jit(solution)/shard_map/all_gather | solution.py:777
  93.3 38.3 %collective-permute-start.19 = (bf16[320,2560]{1,0:T(8,128)(2,1)S(1)}, bf16[320,2560]{1,0:T(8,128)(2,1)}, u32[]{:S(2)}, u32[]{:S(2)}) collective-permute-start(bf16[320,2560]{1,0:T(8,128)(2,1)S(1)} %maximum_maximum_fusion.refs_0_), channel_id=1, source_target_pairs={{0,16},{4,20},{8,24},{12,28},{16,0},{20,4},{24,8},{28,12},{1,17},{... | collective-permute-start | bytes 4915208 | tf_op jit(solution)/shard_map/ppermute | solution.py:568
  94.4 40.3 %collective-permute-start.18 = (bf16[320,2560]{1,0:T(8,128)(2,1)S(1)}, bf16[320,2560]{1,0:T(8,128)(2,1)S(1)}, u32[]{:S(2)}, u32[]{:S(2)}) collective-permute-start(bf16[320,2560]{1,0:T(8,128)(2,1)S(1)} %maximum_maximum_fusion.refs_0_), channel_id=1, source_target_pairs={{0,8},{4,12},{8,0},{12,4},{16,24},{20,28},{24,16},{28,20},{1,9},{5... | collective-permute-start | bytes 4915208 | tf_op jit(solution)/shard_map/ppermute | solution.py:568
  105.4 54.8 %collective-permute-start.17 = (bf16[256,1152]{1,0:T(8,128)(2,1)}, bf16[256,1152]{1,0:T(8,128)(2,1)}, u32[]{:S(2)}, u32[]{:S(2)}) collective-permute-start(bf16[256,1152]{1,0:T(8,128)(2,1)} %get-tuple-element.172.refs_0_), channel_id=1, source_target_pairs={{0,3},{1,0},{2,1},{3,2},{4,7},{5,4},{6,5},{7,6},{8,11},{9,8},{10,9... | collective-permute-start | bytes 1769480 | tf_op jit(solution)/shard_map/ppermute | solution.py:526
  107.7 54.1 %collective-permute-start.16 = (bf16[256,1152]{1,0:T(8,128)(2,1)}, bf16[256,1152]{1,0:T(8,128)(2,1)}, u32[]{:S(2)}, u32[]{:S(2)}) collective-permute-start(bf16[256,1152]{1,0:T(8,128)(2,1)} %get-tuple-element.172.refs_0_), channel_id=1, source_target_pairs={{0,1},{1,2},{2,3},{3,0},{4,5},{5,6},{6,7},{7,4},{8,9},{9,10},{10,1... | collective-permute-start | bytes 1769480 | tf_op jit(solution)/shard_map/ppermute | solution.py:526
  133.7 32.2 %collective-permute-start.23 = (bf16[160,2560]{1,0:T(8,128)(2,1)}, bf16[160,2560]{1,0:T(8,128)(2,1)}, u32[]{:S(2)}, u32[]{:S(2)}) collective-permute-start(bf16[160,2560]{1,0:T(8,128)(2,1)} %slice.245), channel_id=1, source_target_pairs={{0,8},{4,12},{8,0},{12,4},{16,24},{20,28},{24,16},{28,20},{1,9},{5... | collective-permute-start | bytes 2457608 | tf_op jit(solution)/shard_map/ppermute | solution.py:573
  135.7 30.1 %collective-permute-start.22 = (bf16[160,2560]{1,0:T(8,128)(2,1)}, bf16[160,2560]{1,0:T(8,128)(2,1)}, u32[]{:S(2)}, u32[]{:S(2)}) collective-permute-start(bf16[160,2560]{1,0:T(8,128)(2,1)} %slice.244), channel_id=1, source_target_pairs={{0,16},{4,20},{8,24},{12,28},{16,0},{20,4},{24,8},{28,12},{1,17},{... | collective-permute-start | bytes 2457608 | tf_op jit(solution)/shard_map/ppermute | solution.py:573
  196.0 171.9 %all-gather.13.cloned.1.call-start = ((), (), s32[]{:S(2)}) async-start(), calls=%async_computation.11 | async-start | bytes 9584640 | tf_op jit(solution)/shard_map/all_gather | solution.py:778
  228.6 34.6 %all-to-all-start = ((bf16[4,256,640]{2,1,0:T(8,128)(2,1)}), bf16[4,256,640]{2,1,0:T(8,128)(2,1)S(1)}, u32[]{:S(2)}, u32[]{:S(2)}) async-start(bf16[4,256,640]{2,1,0:T(8,128)(2,1)} %bitcast.173), calls=%async_computation | async-start | bytes 2621440 | tf_op jit(solution)/shard_map/all_to_all | solution.py:799
  232.3 276.4 %reduce-scatter.9.cloned.1.call-start = ((), (), s32[]{:S(2)}) async-start(), calls=%async_computation.13 | async-start | bytes 3276800 | tf_op jit(solution)/shard_map/reduce_scatter | solution.py:834
  274.1 29.7 %collective-permute-start.30 = (bf16[128,2560]{1,0:T(8,128)(2,1)S(1)}, bf16[128,2560]{1,0:T(8,128)(2,1)S(1)}, u32[]{:S(2)}, u32[]{:S(2)}) collective-permute-start(bf16[128,2560]{1,0:T(8,128)(2,1)S(1)} %get-tuple-element.333.refs_0_), channel_id=1, source_target_pairs={{0,3},{1,0},{2,1},{3,2},{4,7},{5,4},{6,5},{7,6},{8,11},{9,8},{10,9... | collective-permute-start | bytes 1966088 | tf_op jit(solution)/shard_map/ppermute | solution.py:526
  275.6 29.7 %collective-permute-start.29 = (bf16[128,2560]{1,0:T(8,128)(2,1)S(1)}, bf16[128,2560]{1,0:T(8,128)(2,1)S(1)}, u32[]{:S(2)}, u32[]{:S(2)}) collective-permute-start(bf16[128,2560]{1,0:T(8,128)(2,1)S(1)} %get-tuple-element.333.refs_0_), channel_id=1, source_target_pairs={{0,1},{1,2},{2,3},{3,0},{4,5},{5,6},{6,7},{7,4},{8,9},{9,10},{10,1... | collective-permute-start | bytes 1966088 | tf_op jit(solution)/shard_map/ppermute | solution.py:526
  398.8 109.9 %reduce-scatter.11.cloned.1.call-start = ((), (), s32[]{:S(2)}) async-start(), calls=%async_computation.14 | async-start | bytes 3276800 | tf_op jit(solution)/shard_map/reduce_scatter | solution.py:835
  446.6 367.2 %reduce-scatter.7.cloned.1.call-start = ((), (), s32[]{:S(2)}) async-start(), calls=%async_computation.12 | async-start | bytes 5324800 | tf_op jit(solution)/shard_map/reduce_scatter | solution.py:594
  531.8 40.8 %collective-permute-start.40 = (bf16[4,320,2560]{2,1,0:T(8,128)(2,1)}, bf16[4,320,2560]{2,1,0:T(8,128)(2,1)}, u32[]{:S(2)}, u32[]{:S(2)}) collective-permute-start(bf16[4,320,2560]{2,1,0:T(8,128)(2,1)} %get-tuple-element.229), channel_id=1, source_target_pairs={{0,4},{4,0},{8,12},{12,8},{16,20},{20,16},{24,28},{28,24},{1,5},{5... | collective-permute-start | bytes 19660808 | tf_op jit(solution)/shard_map/ppermute | solution.py:587
  536.2 36.5 %all-to-all-start.1 = ((bf16[4,256,640]{2,1,0:T(8,128)(2,1)}), bf16[4,256,640]{2,1,0:T(8,128)(2,1)}, u32[]{:S(2)}, u32[]{:S(2)}) async-start(bf16[4,256,640]{2,1,0:T(8,128)(2,1)} %fusion.27), calls=%async_computation.4 | async-start | bytes 2621440 | tf_op jit(solution)/shard_map/all_to_all | solution.py:857
  540.5 273.3 %reduce-scatter.15.cloned.1.call-start = ((), (), s32[]{:S(2)}) async-start(), calls=%async_computation.16 | async-start | bytes 3276800 | tf_op jit(solution)/shard_map/reduce_scatter | solution.py:860
  572.7 241.1 %reduce-scatter.17.cloned.1.call-start = ((), (), s32[]{:S(2)}) async-start(), calls=%async_computation.17 | async-start | bytes 3276800 | tf_op jit(solution)/shard_map/reduce_scatter | solution.py:888
  589.6 46.0 %collective-permute-start.42 = (bf16[320,1600]{1,0:T(8,128)(2,1)}, bf16[320,1600]{1,0:T(8,128)(2,1)}, u32[]{:S(2)}, u32[]{:S(2)}) collective-permute-start(bf16[320,1600]{1,0:T(8,128)(2,1)} %side.6), channel_id=1, source_target_pairs={{0,8},{4,12},{8,0},{12,4},{16,24},{20,28},{24,16},{28,20},{1,9},{5... | collective-permute-start | bytes 3072008 | tf_op jit(solution)/shard_map/ppermute | solution.py:689
  595.2 40.5 %collective-permute-start.44 = (bf16[320,1600]{1,0:T(8,128)(2,1)}, bf16[320,1600]{1,0:T(8,128)(2,1)}, u32[]{:S(2)}, u32[]{:S(2)}) collective-permute-start(bf16[320,1600]{1,0:T(8,128)(2,1)} %side.7), channel_id=1, source_target_pairs={{0,16},{4,20},{8,24},{12,28},{16,0},{20,4},{24,8},{28,12},{1,17},{... | collective-permute-start | bytes 3072008 | tf_op jit(solution)/shard_map/ppermute | solution.py:689
  598.8 36.9 %collective-permute-start.45 = (bf16[160,2560]{1,0:T(8,128)(2,1)}, bf16[160,2560]{1,0:T(8,128)(2,1)S(1)}, u32[]{:S(2)}, u32[]{:S(2)}) collective-permute-start(bf16[160,2560]{1,0:T(8,128)(2,1)} %get-tuple-element.245), channel_id=1, source_target_pairs={{0,8},{4,12},{8,0},{12,4},{16,24},{20,28},{24,16},{28,20},{1,9},{5... | collective-permute-start | bytes 2457608 | tf_op jit(solution)/shard_map/ppermute | solution.py:657
  600.4 36.3 %collective-permute-start.46 = (bf16[160,2560]{1,0:T(8,128)(2,1)}, bf16[160,2560]{1,0:T(8,128)(2,1)}, u32[]{:S(2)}, u32[]{:S(2)}) collective-permute-start(bf16[160,2560]{1,0:T(8,128)(2,1)} %get-tuple-element.246), channel_id=1, source_target_pairs={{0,16},{4,20},{8,24},{12,28},{16,0},{20,4},{24,8},{28,12},{1,17},{... | collective-permute-start | bytes 2457608 | tf_op jit(solution)/shard_map/ppermute | solution.py:657
  654.3 47.9 %collective-permute-start.52 = (bf16[320,2560]{1,0:T(8,128)(2,1)}, bf16[320,2560]{1,0:T(8,128)(2,1)}, u32[]{:S(2)}, u32[]{:S(2)}) collective-permute-start(bf16[320,2560]{1,0:T(8,128)(2,1)} %side.8), channel_id=1, source_target_pairs={{0,8},{4,12},{8,0},{12,4},{16,24},{20,28},{24,16},{28,20},{1,9},{5... | collective-permute-start | bytes 4915208 | tf_op jit(solution)/shard_map/ppermute | solution.py:689
  659.1 43.8 %collective-permute-start.53 = (bf16[320,2560]{1,0:T(8,128)(2,1)}, bf16[320,2560]{1,0:T(8,128)(2,1)}, u32[]{:S(2)}, u32[]{:S(2)}) collective-permute-start(bf16[320,2560]{1,0:T(8,128)(2,1)} %side.9), channel_id=1, source_target_pairs={{0,16},{4,20},{8,24},{12,28},{16,0},{20,4},{24,8},{28,12},{1,17},{... | collective-permute-start | bytes 4915208 | tf_op jit(solution)/shard_map/ppermute | solution.py:689
  672.2 30.0 %collective-permute-start.51 = (bf16[4,128,1280]{2,1,0:T(8,128)(2,1)S(1)}, bf16[4,128,1280]{2,1,0:T(8,128)(2,1)}, u32[]{:S(2)}, u32[]{:S(2)}) collective-permute-start(bf16[4,128,1280]{2,1,0:T(8,128)(2,1)S(1)} %fusion.15), channel_id=1, source_target_pairs={{0,4},{4,0},{8,12},{12,8},{16,20},{20,16},{24,28},{28,24},{1,5},{5... | collective-permute-start | bytes 3932168 | tf_op jit(solution)/shard_map/ppermute | solution.py:603
  703.0 137.0 %reduce-scatter.13.cloned.1.call-start = ((), (), s32[]{:S(2)}) async-start(), calls=%async_computation.15 | async-start | bytes 5324800 | tf_op jit(solution)/shard_map/reduce_scatter | solution.py:594
  734.2 33.1 %collective-permute-start.66 = (bf16[320,640]{1,0:T(8,128)(2,1)}, bf16[320,640]{1,0:T(8,128)(2,1)}, u32[]{:S(2)}, u32[]{:S(2)}) collective-permute-start(bf16[320,640]{1,0:T(8,128)(2,1)} %get-tuple-element.329), channel_id=1, source_target_pairs={{0,1},{1,2},{2,3},{3,0},{4,5},{5,6},{6,7},{7,4},{8,9},{9,10},{10,1... | collective-permute-start | bytes 1228808 | tf_op jit(solution)/shard_map/ppermute | solution.py:551
  736.1 43.2 %collective-permute-start.68 = (bf16[320,640]{1,0:T(8,128)(2,1)}, bf16[320,640]{1,0:T(8,128)(2,1)}, u32[]{:S(2)}, u32[]{:S(2)}) collective-permute-start(bf16[320,640]{1,0:T(8,128)(2,1)} %get-tuple-element.330), channel_id=1, source_target_pairs={{0,2},{1,3},{2,0},{3,1},{4,6},{5,7},{6,4},{7,5},{8,10},{9,11},{10,... | collective-permute-start | bytes 1228808 | tf_op jit(solution)/shard_map/ppermute | solution.py:551
  736.5 44.2 %collective-permute-start.67 = (bf16[320,640]{1,0:T(8,128)(2,1)}, bf16[320,640]{1,0:T(8,128)(2,1)}, u32[]{:S(2)}, u32[]{:S(2)}) collective-permute-start(bf16[320,640]{1,0:T(8,128)(2,1)} %get-tuple-element.331), channel_id=1, source_target_pairs={{0,3},{1,0},{2,1},{3,2},{4,7},{5,4},{6,5},{7,6},{8,11},{9,8},{10,9... | collective-permute-start | bytes 1228808 | tf_op jit(solution)/shard_map/ppermute | solution.py:551
  (101 other events, 1402.9 us)
Sparse Core Ops, SparseCore 0:
  10.7 35.8 all-gather.14
  48.2 144.1 all-gather.6
  194.3 53.7 all-gather.8
  249.8 54.9 all-gather.10
  306.5 54.9 all-gather.12
  398.9 51.5 reduce-scatter.8
  452.8 51.7 reduce-scatter.10
  507.6 52.9 reduce-scatter.6
  572.8 50.6 reduce-scatter.14
  703.1 67.4 reduce-scatter.16
  773.6 66.2 reduce-scatter.12
where the time goes:
time: 862 us; the launch traced here: 853 us
  Pallas kernels  324 us (38%)
  waiting for transfers between devices  309 us (36%)
  starting transfers between devices  83.7 us (10%)
  local copies, waits for them, and re-layouts  56.9 us (7%)
  other arithmetic  45.6 us (5%)
  matrix products  17.9 us (2%)
  between operations  15.4 us (2%)
    ppermute x4, waiting for transfers between devices, gather_far(): lax.ppermute(near[2][half:], 'tensor', LEFT)  56.6 us
    pallas_call x4, Pallas kernels, split_gradient(): call(functools.partial(split_kernel, chunks), name, 2 * chunks * tokens *...  54.4 us
    pallas_call x3, Pallas kernels, feed_back(): call(functools.partial(back_kernel, len(lefts), chunks), name, 2 * len(fl...  50.6 us
    ppermute x4, waiting for transfers between devices, gather_near(): lax.ppermute(block, 'tensor', LEFT)  47.3 us
    pallas_call x2, Pallas kernels, feed_forward(): call(functools.partial(feed_kernel, len(feeds)), 'feed_forward', 4 * toke...  33 us
    pallas_call x1, Pallas kernels, local(): call(functools.partial(attention_backward_kernel, block), 'attention_back...  31.4 us
    pallas_call x1, Pallas kernels, local(): call(functools.partial(attention_forward_kernel, rank, block), 'attention...  30.9 us
    pallas_call x2, Pallas kernels, unit_back(): call(functools.partial(unit_kernel, 5), 'unit_back', 2 * tokens * width *...  27.6 us
  transfers between devices with their start and end apart: 82, of which 31 were waited for; matrix products, arithmetic and copies ran while one was open for 12% of the time, Pallas kernels for 34%

commit v1 on v0

--- a/solution.py
+++ b/solution.py
@@ -822,10 +822,12 @@
     else:
         (down_grad,) = weight_gradients("down_gradient", down_lefts, [[inner_0, inner_1]])
         down_core = scatter_core(down_grad.reshape(replicas, -1, down_grad.shape[1]))
+    down_mixed = corner_sum(down_core) if replicas == 8 else down_core
+    down_corner = corner_swap(down_mixed) if replicas == 8 else down_core
     gate_lefts = after_all([feed_0, feed_1], down_grad)
     if replicas == 8:
         gate_own, gate_grad = split_gradient("gate_gradient", gate_lefts, [gate_0, gate_1])
-        upper_own, upper_grad = split_gradient("upper_gradient", after_all(gate_lefts, gate_grad), [upper_0, upper_1])
+        upper_own, upper_grad = split_gradient("upper_gradient", after_all(gate_lefts, gate_grad, *down_mixed), [upper_0, upper_1])
         gate_chips = mix(gate_own, *swap_cores([gate_grad]))
         upper_chips = mix(upper_own, *swap_cores([upper_grad]))
     else:
@@ -833,11 +835,9 @@
         gate_chips, upper_chips = gate_grad, upper_grad
     got_0 = lax.psum_scatter(part_0, "tensor", scatter_dimension=0, tiled=True)
     got_1 = lax.psum_scatter(part_1, "tensor", scatter_dimension=0, tiled=True)
-    down_mixed = corner_sum(down_core) if replicas == 8 else down_core
-    down_corner = corner_swap(down_mixed) if replicas == 8 else down_core
     down_sides = scatter_sides(down_core, down_corner) if replicas == 8 else down_corner
     gate_sum = scatter_chips(gate_chips)
-    got_0, got_1 = after_all([got_0, got_1], gate_chips, upper_chips, *down_mixed)
+    got_0, got_1 = after_all([got_0, got_1], gate_chips, upper_chips, *down_sides)
     feed_in_grad = jnp.concatenate([got_0, got_1]).astype(wide)
 
     feed_gain_part = jnp.sum(feed_in_grad * unit_middle, axis=0, keepdims=True)

time: 862 us -> 857 us (level)
    ppermute x4, waiting for transfers between devices: 12.9 us -> 1.08 us  [corner_swap(): lax.ppermute(corner[1], 'dp', flips(4))]
  transfers between devices with their start and end apart: 82 -> 82, of which waited for: 31 -> 32; matrix products, arithmetic and copies ran while one was open for 12% -> 12% of each run, Pallas kernels for 34% -> 34%
where the time goes in v1:
time: 857 us; the launch traced here: 848 us
  Pallas kernels  323 us (38%)
  waiting for transfers between devices  305 us (36%)
  starting transfers between devices  83.8 us (10%)
  local copies, waits for them, and re-layouts  56.8 us (7%)
  other arithmetic  45.5 us (5%)
  matrix products  18.2 us (2%)
  between operations  15.4 us (2%)
    ppermute x4, waiting for transfers between devices, gather_far(): lax.ppermute(near[2][half:], 'tensor', LEFT)  56.6 us
    pallas_call x4, Pallas kernels, split_gradient(): call(functools.partial(split_kernel, chunks), name, 2 * chunks * tokens *...  54.4 us
    pallas_call x3, Pallas kernels, feed_back(): call(functools.partial(back_kernel, len(lefts), chunks), name, 2 * len(fl...  50.5 us
    ppermute x4, waiting for transfers between devices, gather_near(): lax.ppermute(block, 'tensor', LEFT)  47.2 us
    pallas_call x2, Pallas kernels, feed_forward(): call(functools.partial(feed_kernel, len(feeds)), 'feed_forward', 4 * toke...  32.7 us
    pallas_call x1, Pallas kernels, local(): call(functools.partial(attention_backward_kernel, block), 'attention_back...  31.2 us
    pallas_call x1, Pallas kernels, local(): call(functools.partial(attention_forward_kernel, rank, block), 'attention...  30.9 us
    ppermute x4, waiting for transfers between devices, gather_near(): lax.ppermute(block, 'tensor', RIGHT)  27.8 us
  transfers between devices with their start and end apart: 82, of which 32 were waited for; matrix products, arithmetic and copies ran while one was open for 12% of the time, Pallas kernels for 34%

profile of v1, /device:TPU:0, one launch (start us, length us, event | category | flops | bytes accessed | tf_op | source)
XLA Modules:
  0.0 847.9 jit_solution(3029845755715367672)
XLA Ops:
  45.9 11.7 %collective-permute-done.5 = bf16[320,640]{1,0:T(8,128)(2,1)S(1)} collective-permute-done((bf16[320,640]{1,0:T(8,128)(2,1)S(1)}, bf16[320,640]{1,0:T(8,128)(2,1)S(1)}, u32[]{:S(2)}, u32[]{:S(2)}) %collective-permute-start.5) | collective-permute-done | bytes 409632 | tf_op jit(solution)/shard_map/ppermute | solution.py:526
  65.5 19.9 %collective-permute-done.10 = bf16[160,640]{1,0:T(8,128)(2,1)S(1)} collective-permute-done((bf16[160,640]{1,0:T(8,128)(2,1)S(1)}, bf16[160,640]{1,0:T(8,128)(2,1)S(1)}, u32[]{:S(2)}, u32[]{:S(2)}) %collective-permute-start.10) | collective-permute-done | bytes 204832 | tf_op jit(solution)/shard_map/ppermute | solution.py:531
  95.1 10.1 %down_projections.1 = (bf16[2560,1152]{1,0:T(8,128)(2,1)}, f32[256,1152]{1,0:T(8,128)}, bf16[256,1152]{1,0:T(8,128)(2,1)}, f32[8,2560]{1,0:T(8,128)}) custom-call(s32[10]{0:T(128)} %stack.58.places, bf16[256,2560]{1,0:T(8,128)(2,1)} %hidden.3, bf16[320,1152]{1,0:T(8,128)(2,1)} %place.3.refs_0_, bf16[320,1152]{1,0:T(8,128)(2,1)} %collective-permute-done.3.refs_1_, ...), custom_call_target="tpu_custom_call" | custom-call | tf_op jit(solution)/shard_map/down_projections/pallas_call | solution.py:232
  107.6 24.0 %collective-permute-done.19.refs_2_ = bf16[320,2560]{1,0:T(8,128)(2,1)} collective-permute-done((bf16[320,2560]{1,0:T(8,128)(2,1)S(1)}, bf16[320,2560]{1,0:T(8,128)(2,1)}, u32[]{:S(2)}, u32[]{:S(2)}) %collective-permute-start.19) | collective-permute-done | bytes 1638432 | tf_op jit(solution)/shard_map/ppermute | solution.py:568
  141.4 18.6 %collective-permute-done.17.refs_2_ = bf16[256,1152]{1,0:T(8,128)(2,1)} collective-permute-done((bf16[256,1152]{1,0:T(8,128)(2,1)}, bf16[256,1152]{1,0:T(8,128)(2,1)}, u32[]{:S(2)}, u32[]{:S(2)}) %collective-permute-start.17) | collective-permute-done | bytes 589856 | tf_op jit(solution)/shard_map/ppermute | solution.py:526
  165.7 18.8 %collective-permute-done.21.refs_4_ = bf16[128,1152]{1,0:T(8,128)(2,1)S(1)} collective-permute-done((bf16[128,1152]{1,0:T(8,128)(2,1)S(1)}, bf16[128,1152]{1,0:T(8,128)(2,1)S(1)}, u32[]{:S(2)}, u32[]{:S(2)}) %collective-permute-start.21) | collective-permute-done | bytes 294944 | tf_op jit(solution)/shard_map/ppermute | solution.py:531
  197.6 30.9 %attention_forward.1 = (bf16[1024,640]{1,0:T(8,128)(2,1)}, bf16[1024,1280]{1,0:T(8,128)(2,1)}, bf16[1024,1280]{1,0:T(8,128)(2,1)}, f32[1024,128]{1,0:T(8,128)}) custom-call(bf16[1024,1152]{1,0:T(8,128)(2,1)} %place.4.latents.rotary_in.refs_0_, bf16[768,1280]{1,0:T(8,128)(2,1)} %bitcast.155, bf16[256,1280]{1,0:T(8,128)(2,1)} %bitcast.167, ...), custom_call_target="tpu_custom_call" | custom-call | tf_op jit(solution)/shard_map/attention_forward/pallas_call | solution.py:783
  245.0 9.2 %place.5 = bf16[2560,2560]{1,0:T(8,128)(2,1)} custom-call(bf16[320,2560]{1,0:T(8,128)(2,1)} %copy-done.3, bf16[320,2560]{1,0:T(8,128)(2,1)} %copy-done.10, bf16[320,2560]{1,0:T(8,128)(2,1)} %collective-permute-done.19.refs_2_, bf16[160,2560]{1,0:T(8,128)(2,1)} %collective-permute-done.22.refs_3_, bf16[160,2560]{1,0:T(8,128)(2,1)} %collective-permute-done.23.refs_4_, ...), custom_call_target="tpu_custom_call" | custom-call | tf_op jit(solution)/shard_map/place/pallas_call | solution.py:187
  254.2 8.9 %all-to-all-done = bf16[4,256,640]{2,1,0:T(8,128)(2,1)S(1)} async-done(((bf16[4,256,640]{2,1,0:T(8,128)(2,1)}), bf16[4,256,640]{2,1,0:T(8,128)(2,1)S(1)}, u32[]{:S(2)}, u32[]{:S(2)}) %all-to-all-start) | async-done | bytes 1310752 | tf_op jit(solution)/shard_map/all_to_all | solution.py:799
  264.4 9.2 %multiply_reduce_fusion = (f32[256]{0:T(256)S(1)}, f32[256,2560]{1,0:T(8,128)S(1)}) fusion(bf16[256,2560]{1,0:T(8,128)(2,1)} %pad_maximum_fusion.1.refs_1_, bf16[2560,2560]{1,0:T(8,128)(2,1)} %place.5, bf16[256,2560]{1,0:T(8,128)(2,1)} %hidden.3), kind=kOutput, calls=%fused_computation.30 | convolution fusion | flops 3358719744 | bytes 18351104 | tf_op jit(solution)/shard_map/dot_general | solution.py:15
  276.0 27.6 %collective-permute-done.30.refs_2_ = bf16[128,2560]{1,0:T(8,128)(2,1)S(1)} collective-permute-done((bf16[128,2560]{1,0:T(8,128)(2,1)S(1)}, bf16[128,2560]{1,0:T(8,128)(2,1)S(1)}, u32[]{:S(2)}, u32[]{:S(2)}) %collective-permute-start.30) | collective-permute-done | bytes 655392 | tf_op jit(solution)/shard_map/ppermute | solution.py:526
  307.3 10.6 %collective-permute-done.32.refs_4_ = bf16[64,2560]{1,0:T(8,128)(2,1)S(1)} collective-permute-done((bf16[64,2560]{1,0:T(8,128)(2,1)S(1)}, bf16[64,2560]{1,0:T(8,128)(2,1)S(1)}, u32[]{:S(2)}, u32[]{:S(2)}) %collective-permute-start.32) | collective-permute-done | bytes 327712 | tf_op jit(solution)/shard_map/ppermute | solution.py:531
  320.4 16.3 %feed_forward.2 = (bf16[512,1600]{1,0:T(8,128)(2,1)}, bf16[512,1600]{1,0:T(8,128)(2,1)}, bf16[512,1600]{1,0:T(8,128)(2,1)}, bf16[512,2560]{1,0:T(8,128)(2,1)}) custom-call(bf16[128,2560]{1,0:T(8,128)(2,1)} %copy-done.14, bf16[128,2560]{1,0:T(8,128)(2,1)} %copy-done.20, bf16[128,2560]{1,0:T(8,128)(2,1)} %copy-done.19, bf16[64,2560]{1,0:T(8,128)(2,1)} %copy-done.36, ...), custom_call_target="tpu_custom_call" | custom-call | tf_op jit(solution)/shard_map/feed_forward/pallas_call | solution.py:268
  336.8 13.0 %collective-permute-done.33.refs_1_ = bf16[128,2560]{1,0:T(8,128)(2,1)} collective-permute-done((bf16[128,2560]{1,0:T(8,128)(2,1)S(1)}, bf16[128,2560]{1,0:T(8,128)(2,1)}, u32[]{:S(2)}, u32[]{:S(2)}) %collective-permute-start.33) | collective-permute-done | bytes 655392 | tf_op jit(solution)/shard_map/ppermute | solution.py:526
  368.5 13.7 %unit_back.2 = (bf16[512,1600]{1,0:T(8,128)(2,1)}, bf16[512,1600]{1,0:T(8,128)(2,1)}, bf16[512,2560]{1,0:T(8,128)(2,1)}) custom-call(s32[4]{0:T(128)} %pad_add_fusion.1.places, bf16[1024,2560]{1,0:T(8,128)(2,1)} %all-gather.7.cloned.1.call-done.refs_0_.refs_1_.refs_2_.refs_3_.refs_4_, ...), custom_call_target="tpu_custom_call" | custom-call | tf_op jit(solution)/shard_map/unit_back/pallas_call | solution.py:307
  382.2 17.1 %feed_back.2 = bf16[512,2560]{1,0:T(8,128)(2,1)} custom-call(s32[4]{0:T(128)} %pad_add_fusion.1.places, bf16[512,1600]{1,0:T(8,128)(2,1)} %get-tuple-element.197.refs_0_.refs_2_, bf16[512,1600]{1,0:T(8,128)(2,1)} %get-tuple-element.198.refs_1_.refs_2_, bf16[2560,1600]{1,0:T(8,128)(2,1)} %all-gather.9.cloned.1.call-done.refs_5_.refs_2_, ...), custom_call_target="tpu_custom_call" | custom-call | tf_op jit(solution)/shard_map/feed_back/pallas_call | solution.py:337
  399.4 16.4 %feed_forward.3 = (bf16[512,1600]{1,0:T(8,128)(2,1)}, bf16[512,1600]{1,0:T(8,128)(2,1)}, bf16[512,1600]{1,0:T(8,128)(2,1)}, bf16[512,2560]{1,0:T(8,128)(2,1)}) custom-call(bf16[128,2560]{1,0:T(8,128)(2,1)} %copy-done.13, bf16[128,2560]{1,0:T(8,128)(2,1)} %collective-permute-done.33.refs_1_, bf16[128,2560]{1,0:T(8,128)(2,1)} %collective-permute-done.34.refs_2_, ...), custom_call_target="tpu_custom_call" | custom-call | tf_op jit(solution)/shard_map/feed_forward/pallas_call | solution.py:268
  415.8 13.7 %unit_back.3 = (bf16[512,1600]{1,0:T(8,128)(2,1)}, bf16[512,1600]{1,0:T(8,128)(2,1)}, bf16[512,2560]{1,0:T(8,128)(2,1)}) custom-call(s32[4]{0:T(128)} %pad_add_fusion.1.places, bf16[1024,2560]{1,0:T(8,128)(2,1)} %all-gather.7.cloned.1.call-done.refs_0_.refs_1_.refs_2_.refs_3_.refs_4_, ...), custom_call_target="tpu_custom_call" | custom-call | tf_op jit(solution)/shard_map/unit_back/pallas_call | solution.py:307
  429.5 17.1 %feed_back.3 = bf16[512,2560]{1,0:T(8,128)(2,1)} custom-call(s32[4]{0:T(128)} %pad_add_fusion.1.places, bf16[512,1600]{1,0:T(8,128)(2,1)} %get-tuple-element.209.refs_0_.refs_3_, bf16[512,1600]{1,0:T(8,128)(2,1)} %get-tuple-element.210.refs_1_.refs_3_, bf16[2560,1600]{1,0:T(8,128)(2,1)} %all-gather.9.cloned.1.call-done.refs_5_.refs_2_, ...), custom_call_target="tpu_custom_call" | custom-call | tf_op jit(solution)/shard_map/feed_back/pallas_call | solution.py:337
  446.6 14.9 %down_gradient.1 = (bf16[4,320,1600]{2,1,0:T(8,128)(2,1)}, bf16[4,320,1600]{2,1,0:T(8,128)(2,1)}) custom-call(s32[1]{0:T(128)S(6)} %select_n.206.core, bf16[512,2560]{1,0:T(8,128)(2,1)} %get-tuple-element.211.refs_0_, bf16[512,2560]{1,0:T(8,128)(2,1)} %get-tuple-element.212.refs_1_, bf16[512,1600]{1,0:T(8,128)(2,1)} %get-tuple-element.231.refs_2_.refs_0_, ...), custom_call_target="tpu_custom_call" | custom-call | tf_op jit(solution)/shard_map/down_gradient/pallas_call | solution.py:402
  461.8 15.0 %gate_gradient.1 = (bf16[4,320,1600]{2,1,0:T(8,128)(2,1)}, bf16[4,320,1600]{2,1,0:T(8,128)(2,1)}) custom-call(s32[1]{0:T(128)S(6)} %select_n.206.core, bf16[512,2560]{1,0:T(8,128)(2,1)} %get-tuple-element.222.refs_0_, bf16[512,2560]{1,0:T(8,128)(2,1)} %get-tuple-element.223.refs_1_, bf16[512,1600]{1,0:T(8,128)(2,1)} %get-tuple-element.197.refs_0_.refs_2_, ...), custom_call_target="tpu_custom_call" | custom-call | tf_op jit(solution)/shard_map/gate_gradient/pallas_call | solution.py:402
  480.0 15.1 %upper_gradient.1 = (bf16[4,320,1600]{2,1,0:T(8,128)(2,1)}, bf16[4,320,1600]{2,1,0:T(8,128)(2,1)}) custom-call(s32[1]{0:T(128)S(6)} %select_n.206.core, bf16[512,2560]{1,0:T(8,128)(2,1)} %get-tuple-element.222.refs_0_, bf16[512,2560]{1,0:T(8,128)(2,1)} %get-tuple-element.223.refs_1_, bf16[512,1600]{1,0:T(8,128)(2,1)} %get-tuple-element.198.refs_1_.refs_2_, ...), custom_call_target="tpu_custom_call" | custom-call | tf_op jit(solution)/shard_map/upper_gradient/pallas_call | solution.py:402
  527.8 9.0 %convolution_convert_fusion = bf16[256,2560]{1,0:T(8,128)(2,1)S(1)} fusion(bf16[256,2560]{1,0:T(8,128)(2,1)S(1)} %get-tuple-element.228.refs_0_, bf16[2560,2560]{1,0:T(8,128)(2,1)} %place.5), kind=kOutput, calls=%fused_computation.9 | convolution fusion | flops 3356098560 | bytes 15728640 | tf_op jit(solution)/shard_map/dot_general | solution.py:19
  536.8 9.3 %out_gradient.1 = (bf16[4,320,2560]{2,1,0:T(8,128)(2,1)}, bf16[4,320,2560]{2,1,0:T(8,128)(2,1)}) custom-call(s32[1]{0:T(128)S(6)} %select_n.206.core, bf16[256,2560]{1,0:T(8,128)(2,1)} %copy-done.9, bf16[256,2560]{1,0:T(8,128)(2,1)} %pad_maximum_fusion.1.refs_1_), custom_call_target="tpu_custom_call" | custom-call | tf_op jit(solution)/shard_map/out_gradient/pallas_call | solution.py:402
  554.7 16.3 %branch_two.1 = (bf16[512,2560]{1,0:T(8,128)(2,1)}, bf16[512,2560]{1,0:T(8,128)(2,1)}) custom-call(s32[4]{0:T(128)} %pad_add_fusion.1.places, bf16[512,1600]{1,0:T(8,128)(2,1)} %get-tuple-element.231.refs_2_.refs_0_, bf16[512,1600]{1,0:T(8,128)(2,1)} %get-tuple-element.232.refs_3_.refs_1_, bf16[2560,1600]{1,0:T(8,128)(2,1)} %all-gather.13.cloned.1.call-done.refs_7_.refs_2_), custom_call_target="tpu_custom_call" | custom-call | tf_op jit(solution)/shard_map/branch_two/pallas_call | solution.py:337
  571.0 16.0 %all-to-all-done.1 = bf16[4,256,640]{2,1,0:T(8,128)(2,1)} async-done(((bf16[4,256,640]{2,1,0:T(8,128)(2,1)}), bf16[4,256,640]{2,1,0:T(8,128)(2,1)}, u32[]{:S(2)}, u32[]{:S(2)}) %all-to-all-start.1) | async-done | bytes 1310752 | tf_op jit(solution)/shard_map/all_to_all | solution.py:857
  598.0 31.2 %attention_backward.1 = (bf16[1024,1280]{1,0:T(8,128)(2,1)}, bf16[1024,1280]{1,0:T(8,128)(2,1)}, f32[1024,128]{1,0:T(8,128)}) custom-call(bf16[1024,1280]{1,0:T(8,128)(2,1)} %get-tuple-element.239.queries, bf16[1024,1280]{1,0:T(8,128)(2,1)} %get-tuple-element.240.expanded, bf16[1024,1152]{1,0:T(8,128)(2,1)} %place.4.latents.rotary_in.refs_0_, ...), custom_call_target="tpu_custom_call" | custom-call | tf_op jit(solution)/shard_map/attention_backward/pallas_call | solution.py:865
  670.5 13.7 %collective-permute-done.48.one = bf16[256,1152]{1,0:T(8,128)(2,1)S(1)} collective-permute-done((bf16[256,1152]{1,0:T(8,128)(2,1)S(1)}, bf16[256,1152]{1,0:T(8,128)(2,1)S(1)}, u32[]{:S(2)}, u32[]{:S(2)}) %collective-permute-start.48) | collective-permute-done | bytes 589856 | tf_op jit(solution)/shard_map/ppermute | solution.py:542
  684.2 12.9 %collective-permute-done.50.two = bf16[256,1152]{1,0:T(8,128)(2,1)S(1)} collective-permute-done((bf16[256,1152]{1,0:T(8,128)(2,1)S(1)}, bf16[256,1152]{1,0:T(8,128)(2,1)S(1)}, u32[]{:S(2)}, u32[]{:S(2)}) %collective-permute-start.50) | collective-permute-done | bytes 589856 | tf_op jit(solution)/shard_map/ppermute | solution.py:542
  704.8 15.7 %input_back.1 = (bf16[4,320,1152]{2,1,0:T(8,128)(2,1)}, bf16[4,320,1152]{2,1,0:T(8,128)(2,1)}, bf16[256,2560]{1,0:T(8,128)(2,1)}) custom-call(s32[1]{0:T(128)S(6)} %select_n.206.core, bf16[256,1152]{1,0:T(8,128)(2,1)} %dynamic-slice_bitcast_fusion.own, bf16[256,1152]{1,0:T(8,128)(2,1)} %copy-done.27, bf16[256,1152]{1,0:T(8,128)(2,1)} %copy-done.28, ...), custom_call_target="tpu_custom_call" | custom-call | tf_op jit(solution)/shard_map/input_back/pallas_call | solution.py:501
  763.0 11.0 %collective-permute-done.68 = bf16[320,640]{1,0:T(8,128)(2,1)} collective-permute-done((bf16[320,640]{1,0:T(8,128)(2,1)}, bf16[320,640]{1,0:T(8,128)(2,1)}, u32[]{:S(2)}, u32[]{:S(2)}) %collective-permute-start.68) | collective-permute-done | bytes 409632 | tf_op jit(solution)/shard_map/ppermute | solution.py:551
  808.5 26.2 %reduce-scatter.13.cloned.1.call-done = bf16[320,1600]{1,0:T(8,128)(2,1)} async-done(((bf16[1280,1600]{1,0:T(8,128)(2,1)}), bf16[320,1600]{1,0:T(8,128)(2,1)}) %reduce-scatter.13.cloned.1.call-update) | async-done | bytes 1024016 | tf_op jit(solution)/shard_map/reduce_scatter | solution.py:594
  (384 shorter events, 319.2 us)
Async XLA Ops:
  7.2 128.9 %all-gather.15.cloned.1.call-start = ((), (), s32[]{:S(2)}) async-start(), calls=%async_computation.18 | async-start | bytes 2949120 | tf_op jit(solution)/shard_map/all_gather | solution.py:726
  10.6 253.8 %all-gather.7.cloned.1.call-start = ((), (), s32[]{:S(2)}) async-start(), calls=%async_computation.8 | async-start | bytes 6553600 | tf_op jit(solution)/shard_map/all_gather | solution.py:730
  11.3 309.0 %all-gather.9.cloned.1.call-start = ((), (), s32[]{:S(2)}) async-start(), calls=%async_computation.9 | async-start | bytes 9584640 | tf_op jit(solution)/shard_map/all_gather | solution.py:755
  91.6 228.8 %all-gather.11.cloned.1.call-start = ((), (), s32[]{:S(2)}) async-start(), calls=%async_computation.10 | async-start | bytes 9584640 | tf_op jit(solution)/shard_map/all_gather | solution.py:777
  93.3 38.3 %collective-permute-start.19 = (bf16[320,2560]{1,0:T(8,128)(2,1)S(1)}, bf16[320,2560]{1,0:T(8,128)(2,1)}, u32[]{:S(2)}, u32[]{:S(2)}) collective-permute-start(bf16[320,2560]{1,0:T(8,128)(2,1)S(1)} %maximum_maximum_fusion.refs_0_), channel_id=1, source_target_pairs={{0,16},{4,20},{8,24},{12,28},{16,0},{20,4},{24,8},{28,12},{1,17},{... | collective-permute-start | bytes 4915208 | tf_op jit(solution)/shard_map/ppermute | solution.py:568
  94.4 40.3 %collective-permute-start.18 = (bf16[320,2560]{1,0:T(8,128)(2,1)S(1)}, bf16[320,2560]{1,0:T(8,128)(2,1)S(1)}, u32[]{:S(2)}, u32[]{:S(2)}) collective-permute-start(bf16[320,2560]{1,0:T(8,128)(2,1)S(1)} %maximum_maximum_fusion.refs_0_), channel_id=1, source_target_pairs={{0,8},{4,12},{8,0},{12,4},{16,24},{20,28},{24,16},{28,20},{1,9},{5... | collective-permute-start | bytes 4915208 | tf_op jit(solution)/shard_map/ppermute | solution.py:568
  105.2 54.9 %collective-permute-start.17 = (bf16[256,1152]{1,0:T(8,128)(2,1)}, bf16[256,1152]{1,0:T(8,128)(2,1)}, u32[]{:S(2)}, u32[]{:S(2)}) collective-permute-start(bf16[256,1152]{1,0:T(8,128)(2,1)} %get-tuple-element.172.refs_0_), channel_id=1, source_target_pairs={{0,3},{1,0},{2,1},{3,2},{4,7},{5,4},{6,5},{7,6},{8,11},{9,8},{10,9... | collective-permute-start | bytes 1769480 | tf_op jit(solution)/shard_map/ppermute | solution.py:526
  107.6 54.0 %collective-permute-start.16 = (bf16[256,1152]{1,0:T(8,128)(2,1)}, bf16[256,1152]{1,0:T(8,128)(2,1)}, u32[]{:S(2)}, u32[]{:S(2)}) collective-permute-start(bf16[256,1152]{1,0:T(8,128)(2,1)} %get-tuple-element.172.refs_0_), channel_id=1, source_target_pairs={{0,1},{1,2},{2,3},{3,0},{4,5},{5,6},{6,7},{7,4},{8,9},{9,10},{10,1... | collective-permute-start | bytes 1769480 | tf_op jit(solution)/shard_map/ppermute | solution.py:526
  133.7 32.0 %collective-permute-start.23 = (bf16[160,2560]{1,0:T(8,128)(2,1)}, bf16[160,2560]{1,0:T(8,128)(2,1)}, u32[]{:S(2)}, u32[]{:S(2)}) collective-permute-start(bf16[160,2560]{1,0:T(8,128)(2,1)} %slice.245), channel_id=1, source_target_pairs={{0,8},{4,12},{8,0},{12,4},{16,24},{20,28},{24,16},{28,20},{1,9},{5... | collective-permute-start | bytes 2457608 | tf_op jit(solution)/shard_map/ppermute | solution.py:573
  135.7 30.0 %collective-permute-start.22 = (bf16[160,2560]{1,0:T(8,128)(2,1)}, bf16[160,2560]{1,0:T(8,128)(2,1)}, u32[]{:S(2)}, u32[]{:S(2)}) collective-permute-start(bf16[160,2560]{1,0:T(8,128)(2,1)} %slice.244), channel_id=1, source_target_pairs={{0,16},{4,20},{8,24},{12,28},{16,0},{20,4},{24,8},{28,12},{1,17},{... | collective-permute-start | bytes 2457608 | tf_op jit(solution)/shard_map/ppermute | solution.py:573
  196.0 172.5 %all-gather.13.cloned.1.call-start = ((), (), s32[]{:S(2)}) async-start(), calls=%async_computation.11 | async-start | bytes 9584640 | tf_op jit(solution)/shard_map/all_gather | solution.py:778
  228.6 34.5 %all-to-all-start = ((bf16[4,256,640]{2,1,0:T(8,128)(2,1)}), bf16[4,256,640]{2,1,0:T(8,128)(2,1)S(1)}, u32[]{:S(2)}, u32[]{:S(2)}) async-start(bf16[4,256,640]{2,1,0:T(8,128)(2,1)} %bitcast.173), calls=%async_computation | async-start | bytes 2621440 | tf_op jit(solution)/shard_map/all_to_all | solution.py:799
  232.3 290.5 %reduce-scatter.9.cloned.1.call-start = ((), (), s32[]{:S(2)}) async-start(), calls=%async_computation.13 | async-start | bytes 3276800 | tf_op jit(solution)/shard_map/reduce_scatter | solution.py:836
  274.0 29.7 %collective-permute-start.30 = (bf16[128,2560]{1,0:T(8,128)(2,1)S(1)}, bf16[128,2560]{1,0:T(8,128)(2,1)S(1)}, u32[]{:S(2)}, u32[]{:S(2)}) collective-permute-start(bf16[128,2560]{1,0:T(8,128)(2,1)S(1)} %get-tuple-element.333.refs_0_), channel_id=1, source_target_pairs={{0,3},{1,0},{2,1},{3,2},{4,7},{5,4},{6,5},{7,6},{8,11},{9,8},{10,9... | collective-permute-start | bytes 1966088 | tf_op jit(solution)/shard_map/ppermute | solution.py:526
  275.5 29.7 %collective-permute-start.29 = (bf16[128,2560]{1,0:T(8,128)(2,1)S(1)}, bf16[128,2560]{1,0:T(8,128)(2,1)S(1)}, u32[]{:S(2)}, u32[]{:S(2)}) collective-permute-start(bf16[128,2560]{1,0:T(8,128)(2,1)S(1)} %get-tuple-element.333.refs_0_), channel_id=1, source_target_pairs={{0,1},{1,2},{2,3},{3,0},{4,5},{5,6},{6,7},{7,4},{8,9},{9,10},{10,1... | collective-permute-start | bytes 1966088 | tf_op jit(solution)/shard_map/ppermute | solution.py:526
  399.3 123.4 %reduce-scatter.11.cloned.1.call-start = ((), (), s32[]{:S(2)}) async-start(), calls=%async_computation.14 | async-start | bytes 3276800 | tf_op jit(solution)/shard_map/reduce_scatter | solution.py:837
  461.6 346.9 %reduce-scatter.7.cloned.1.call-start = ((), (), s32[]{:S(2)}) async-start(), calls=%async_computation.12 | async-start | bytes 5324800 | tf_op jit(solution)/shard_map/reduce_scatter | solution.py:594
  546.2 40.9 %collective-permute-start.42 = (bf16[4,320,2560]{2,1,0:T(8,128)(2,1)}, bf16[4,320,2560]{2,1,0:T(8,128)(2,1)}, u32[]{:S(2)}, u32[]{:S(2)}) collective-permute-start(bf16[4,320,2560]{2,1,0:T(8,128)(2,1)} %get-tuple-element.229), channel_id=1, source_target_pairs={{0,4},{4,0},{8,12},{12,8},{16,20},{20,16},{24,28},{28,24},{1,5},{5... | collective-permute-start | bytes 19660808 | tf_op jit(solution)/shard_map/ppermute | solution.py:587
  550.3 36.7 %all-to-all-start.1 = ((bf16[4,256,640]{2,1,0:T(8,128)(2,1)}), bf16[4,256,640]{2,1,0:T(8,128)(2,1)}, u32[]{:S(2)}, u32[]{:S(2)}) async-start(bf16[4,256,640]{2,1,0:T(8,128)(2,1)} %fusion.27), calls=%async_computation.4 | async-start | bytes 2621440 | tf_op jit(solution)/shard_map/all_to_all | solution.py:857
  554.6 253.9 %reduce-scatter.15.cloned.1.call-start = ((), (), s32[]{:S(2)}) async-start(), calls=%async_computation.16 | async-start | bytes 3276800 | tf_op jit(solution)/shard_map/reduce_scatter | solution.py:860
  587.1 221.4 %reduce-scatter.17.cloned.1.call-start = ((), (), s32[]{:S(2)}) async-start(), calls=%async_computation.17 | async-start | bytes 3276800 | tf_op jit(solution)/shard_map/reduce_scatter | solution.py:888
  587.1 42.1 %collective-permute-start.43 = (bf16[320,1600]{1,0:T(8,128)(2,1)}, bf16[320,1600]{1,0:T(8,128)(2,1)}, u32[]{:S(2)}, u32[]{:S(2)}) collective-permute-start(bf16[320,1600]{1,0:T(8,128)(2,1)} %side.6), channel_id=1, source_target_pairs={{0,8},{4,12},{8,0},{12,4},{16,24},{20,28},{24,16},{28,20},{1,9},{5... | collective-permute-start | bytes 3072008 | tf_op jit(solution)/shard_map/ppermute | solution.py:689
  588.5 40.7 %collective-permute-start.44 = (bf16[320,1600]{1,0:T(8,128)(2,1)}, bf16[320,1600]{1,0:T(8,128)(2,1)}, u32[]{:S(2)}, u32[]{:S(2)}) collective-permute-start(bf16[320,1600]{1,0:T(8,128)(2,1)} %side.7), channel_id=1, source_target_pairs={{0,16},{4,20},{8,24},{12,28},{16,0},{20,4},{24,8},{28,12},{1,17},{... | collective-permute-start | bytes 3072008 | tf_op jit(solution)/shard_map/ppermute | solution.py:689
  592.4 37.7 %collective-permute-start.45 = (bf16[160,2560]{1,0:T(8,128)(2,1)}, bf16[160,2560]{1,0:T(8,128)(2,1)S(1)}, u32[]{:S(2)}, u32[]{:S(2)}) collective-permute-start(bf16[160,2560]{1,0:T(8,128)(2,1)} %get-tuple-element.245), channel_id=1, source_target_pairs={{0,8},{4,12},{8,0},{12,4},{16,24},{20,28},{24,16},{28,20},{1,9},{5... | collective-permute-start | bytes 2457608 | tf_op jit(solution)/shard_map/ppermute | solution.py:657
  593.8 37.4 %collective-permute-start.46 = (bf16[160,2560]{1,0:T(8,128)(2,1)}, bf16[160,2560]{1,0:T(8,128)(2,1)}, u32[]{:S(2)}, u32[]{:S(2)}) collective-permute-start(bf16[160,2560]{1,0:T(8,128)(2,1)} %get-tuple-element.246), channel_id=1, source_target_pairs={{0,16},{4,20},{8,24},{12,28},{16,0},{20,4},{24,8},{28,12},{1,17},{... | collective-permute-start | bytes 2457608 | tf_op jit(solution)/shard_map/ppermute | solution.py:657
  649.0 48.1 %collective-permute-start.52 = (bf16[320,2560]{1,0:T(8,128)(2,1)}, bf16[320,2560]{1,0:T(8,128)(2,1)}, u32[]{:S(2)}, u32[]{:S(2)}) collective-permute-start(bf16[320,2560]{1,0:T(8,128)(2,1)} %side.8), channel_id=1, source_target_pairs={{0,8},{4,12},{8,0},{12,4},{16,24},{20,28},{24,16},{28,20},{1,9},{5... | collective-permute-start | bytes 4915208 | tf_op jit(solution)/shard_map/ppermute | solution.py:689
  653.5 44.3 %collective-permute-start.53 = (bf16[320,2560]{1,0:T(8,128)(2,1)}, bf16[320,2560]{1,0:T(8,128)(2,1)}, u32[]{:S(2)}, u32[]{:S(2)}) collective-permute-start(bf16[320,2560]{1,0:T(8,128)(2,1)} %side.9), channel_id=1, source_target_pairs={{0,16},{4,20},{8,24},{12,28},{16,0},{20,4},{24,8},{28,12},{1,17},{... | collective-permute-start | bytes 4915208 | tf_op jit(solution)/shard_map/ppermute | solution.py:689
  667.2 29.8 %collective-permute-start.51 = (bf16[4,128,1280]{2,1,0:T(8,128)(2,1)S(1)}, bf16[4,128,1280]{2,1,0:T(8,128)(2,1)}, u32[]{:S(2)}, u32[]{:S(2)}) collective-permute-start(bf16[4,128,1280]{2,1,0:T(8,128)(2,1)S(1)} %fusion.15), channel_id=1, source_target_pairs={{0,4},{4,0},{8,12},{12,8},{16,20},{20,16},{24,28},{28,24},{1,5},{5... | collective-permute-start | bytes 3932168 | tf_op jit(solution)/shard_map/ppermute | solution.py:603
  697.9 136.8 %reduce-scatter.13.cloned.1.call-start = ((), (), s32[]{:S(2)}) async-start(), calls=%async_computation.15 | async-start | bytes 5324800 | tf_op jit(solution)/shard_map/reduce_scatter | solution.py:594
  728.7 33.2 %collective-permute-start.66 = (bf16[320,640]{1,0:T(8,128)(2,1)}, bf16[320,640]{1,0:T(8,128)(2,1)}, u32[]{:S(2)}, u32[]{:S(2)}) collective-permute-start(bf16[320,640]{1,0:T(8,128)(2,1)} %get-tuple-element.329), channel_id=1, source_target_pairs={{0,1},{1,2},{2,3},{3,0},{4,5},{5,6},{6,7},{7,4},{8,9},{9,10},{10,1... | collective-permute-start | bytes 1228808 | tf_op jit(solution)/shard_map/ppermute | solution.py:551
  730.4 43.5 %collective-permute-start.68 = (bf16[320,640]{1,0:T(8,128)(2,1)}, bf16[320,640]{1,0:T(8,128)(2,1)}, u32[]{:S(2)}, u32[]{:S(2)}) collective-permute-start(bf16[320,640]{1,0:T(8,128)(2,1)} %get-tuple-element.330), channel_id=1, source_target_pairs={{0,2},{1,3},{2,0},{3,1},{4,6},{5,7},{6,4},{7,5},{8,10},{9,11},{10,... | collective-permute-start | bytes 1228808 | tf_op jit(solution)/shard_map/ppermute | solution.py:551
  731.0 44.5 %collective-permute-start.67 = (bf16[320,640]{1,0:T(8,128)(2,1)}, bf16[320,640]{1,0:T(8,128)(2,1)}, u32[]{:S(2)}, u32[]{:S(2)}) collective-permute-start(bf16[320,640]{1,0:T(8,128)(2,1)} %get-tuple-element.331), channel_id=1, source_target_pairs={{0,3},{1,0},{2,1},{3,2},{4,7},{5,4},{6,5},{7,6},{8,11},{9,8},{10,9... | collective-permute-start | bytes 1228808 | tf_op jit(solution)/shard_map/ppermute | solution.py:551
  (101 other events, 1427.0 us)
Sparse Core Ops, SparseCore 0:
  10.7 35.9 all-gather.14
  48.2 144.2 all-gather.6
  194.4 53.6 all-gather.8
  249.8 54.9 all-gather.10
  306.5 54.9 all-gather.12
  399.5 50.3 reduce-scatter.8
  461.7 50.6 reduce-scatter.10
  515.4 52.9 reduce-scatter.6
  587.2 50.1 reduce-scatter.14
  698.0 67.4 reduce-scatter.16
  768.5 66.1 reduce-scatter.12
